TPU v7x, 32 devices: a whole 2x2x4 slice. The times are simulated.
32 devices in a mesh: expert: 8 (over z, x), wshard: 4 (over y, core).
Axes of the slice: x: 2, y: 2, z: 4, core: 2. Of those that a mesh axis runs over, the one named last changes fastest.
Arguments:
- images: bfloat16 [12608, 512], P(('expert', 'wshard')), may hold values from -6 to 6
- attn_in: bfloat16 [2, 512, 1536], P(None, 'wshard'), may hold values from -0.25 to 0.25
- attn_out: bfloat16 [2, 512, 512], P(None, 'wshard'), may hold values from -0.75 to 0.75
- norm_gains: bfloat16 [4, 512], P(None, 'wshard'), may hold values from 0.5 to 1.5
- mlp_in: bfloat16 [512, 2048], P('wshard'), may hold values from -0.25 to 0.25
- mlp_out: bfloat16 [2048, 512], P('wshard'), may hold values from -0.1875 to 0.1875
- router: bfloat16 [512, 8], P('wshard'), may hold values from -0.1875 to 0.1875
- expert_in: bfloat16 [8, 512, 2048], P('expert'), may hold values from -0.25 to 0.25
- expert_out: bfloat16 [8, 2048, 512], P('expert'), may hold values from -0.25 to 0.25
- expert_ids: int32 [12608, 2], P(('expert', 'wshard')), may hold values from 0 to 7, all different within a row; in each aligned block of 394 rows (0 to 393, 394 to 787, ...) at most 197 rows name the same one
- cotangent: bfloat16 [12608, 512], P(('expert', 'wshard')), may hold values from -6 to 6
Outputs:
- final: bfloat16 [12608, 512], P(('expert', 'wshard'))
- images_grad: float32 [12608, 512], P(('expert', 'wshard'))
- attn_in_grad: float32 [2, 512, 1536], P(None, 'wshard')
- attn_out_grad: float32 [2, 512, 512], P(None, 'wshard')
- norm_gains_grad: float32 [4, 512], P(None, 'wshard')
- mlp_in_grad: float32 [512, 2048], P('wshard')
- mlp_out_grad: float32 [2048, 512], P('wshard')
- router_grad: float32 [512, 8], P('wshard')
- expert_in_grad: float32 [8, 512, 2048], P('expert')
- expert_out_grad: float32 [8, 2048, 512], P('expert')
Inputs may be any that keep to these rules, and one draw needn't show every extreme that they name: `expert_ids`: each token names 2 different experts. The rows of one device name no expert more than 197 times, and in some device's rows one expert is named exactly 197 times.
All inputs are finite; a program needn't handle non-finite values.
Results may differ from a plain program's by a relative error of at most 0.023.
Values may be sent and summed in bfloat16 or wider, within the bound.
No kernel may reach another device: no remote copies, remote signals or barrier semaphores. Data moves between devices by JAX's collectives and lax.ppermute only.
A program may use at most 192 MiB of HBM per device.

v0:
```python
import functools

import jax
import jax.numpy as jnp
from jax import lax
from jax.experimental import pallas as pl
from jax.experimental.pallas import tpu as pltpu
from jax.sharding import PartitionSpec as P

D = 512
HEADS = 8
FF = 2048
SEQ = 197
TOP = 2
HEAD_DIM = 64
PAD = 208
STRIP = 32
CHUNK = 512
EPSILON = 1e-06
ROOT_2_PI = 0.7978845608028654
CUBIC = 0.044715

F32 = jnp.float32
BF16 = jnp.bfloat16
VMEM_LIMIT = 40 * 1024 * 1024
LINKED = 8


def dot(a, b, ca=1, cb=0):
    return lax.dot_general(a, b, (((ca,), (cb,)), ((), ())), preferred_element_type=F32)


def unit_rows(rows):
    centred = rows - jnp.mean(rows, axis=-1, keepdims=True)
    scale = lax.rsqrt(jnp.mean(centred * centred, axis=-1, keepdims=True) + EPSILON)
    return centred * scale, scale


def norm_backward(unit, scale, gain, grad):
    scaled = gain * grad
    inner = (
        scaled
        - jnp.mean(scaled, axis=-1, keepdims=True)
        - unit * jnp.mean(scaled * unit, axis=-1, keepdims=True)
    )
    return inner * scale, jnp.sum(grad * unit, axis=0, keepdims=True)


def gelu_parts(h):
    square = h * h
    t = jnp.tanh(ROOT_2_PI * h * (1.0 + CUBIC * square))
    half = 0.5 * (1.0 + t)
    slope = half + 0.5 * h * (1.0 - t * t) * (ROOT_2_PI * (1.0 + 3.0 * CUBIC * square))
    return h * half, slope


def gelu(h):
    return 0.5 * h * (1.0 + jnp.tanh(ROOT_2_PI * h * (1.0 + CUBIC * h * h)))


def start_weight(pos_ref, pieces, held, sems, first):
    copies = []
    for j, piece in enumerate(pieces):
        copy = pltpu.make_async_copy(piece, held.at[pos_ref[0] ^ j], sems.at[first + j])
        copy.start()
        copies.append(copy)
    return copies


def wait_all(copies):
    for copy in copies:
        copy.wait()


def softmax_rows(q, k):
    scores = dot(q, k, 1, 1) * (HEAD_DIM**-0.5)
    column = lax.broadcasted_iota(jnp.int32, scores.shape, 1)
    scores = jnp.where(column < SEQ, scores, -1e30)
    raised = jnp.exp(scores - jnp.max(scores, axis=-1, keepdims=True))
    return raised * (1.0 / jnp.sum(raised, axis=-1, keepdims=True))


def shards_of(pos_ref, send_ref, keep_ref):
    for target, turn in ((send_ref, 1), (keep_ref, 0)):
        for place in range(2):
            yield target, place, pos_ref[0] ^ (turn + 2 * (1 - place))


def own_half(pos_ref, half):
    return 1 - ((pos_ref[1] & 1) ^ half)


def attend_forward_kernel(pos_ref, x_ref, gain_ref, *refs):
    wi, wo = refs[0:4], refs[4:8]
    y_ref, packed_ref, o_ref, wi_held, wo_held, sems = refs[8:]
    wi_copies = start_weight(pos_ref, wi, wi_held, sems, 0)
    wo_copies = start_weight(pos_ref, wo, wo_held, sems, 4)
    rows = x_ref[...].astype(F32)
    unit, _ = unit_rows(rows)
    normed = (unit * gain_ref[...]).astype(BF16)
    wait_all(wi_copies)
    packed_ref[...] = dot(normed, wi_held[...].reshape(D, 3 * D)).astype(BF16)
    lane = lax.broadcasted_iota(jnp.int32, (PAD, 2 * HEAD_DIM), 1)
    for image in range(x_ref.shape[0] // PAD):
        here = pl.ds(image * PAD, PAD)
        for pair in range(HEADS // 2):
            at = pair * 2 * HEAD_DIM
            q = packed_ref[here, at : at + 128]
            k = packed_ref[here, D + at : D + at + 128]
            v = packed_ref[here, 2 * D + at : 2 * D + at + 128]
            total = None
            for side in range(2):
                mine = (lane >= HEAD_DIM) == bool(side)
                chances = softmax_rows(jnp.where(mine, q, jnp.zeros_like(q)), k).astype(BF16)
                part = dot(chances, jnp.where(mine, v, jnp.zeros_like(v)))
                total = part if total is None else total + part
            o_ref[here, at : at + 128] = total.astype(BF16)
    wait_all(wo_copies)
    y_ref[...] = x_ref[...].astype(F32) + dot(o_ref[...], wo_held[...].reshape(D, D))


def attend_backward_kernel(smalls, pos_ref, x_ref, gain_ref, packed_ref, o_ref, dz_ref, *refs):
    wi, wo = refs[0:4], refs[4:8]
    extra = refs[8 : 8 + smalls]
    dx_ref, dgain_ref, send_ref, keep_ref, wi_held, wo_held, dp_ref, dout_ref, do_ref, normed_ref, sems = refs[
        8 + smalls :
    ]
    wo_copies = start_weight(pos_ref, wo, wo_held, sems, 4)
    wi_copies = start_weight(pos_ref, wi, wi_held, sems, 0)
    unit, scale = unit_rows(x_ref[...].astype(F32))
    gain = gain_ref[...]
    normed_ref[...] = (unit * gain).astype(BF16)
    dout_ref[...] = dz_ref[...].astype(BF16)
    wait_all(wo_copies)
    do_ref[...] = dot(dout_ref[...], wo_held[...].reshape(D, D), 1, 1).astype(BF16)
    lane = lax.broadcasted_iota(jnp.int32, (PAD, 2 * HEAD_DIM), 1)
    factor = HEAD_DIM**-0.5
    for image in range(x_ref.shape[0] // PAD):
        here = pl.ds(image * PAD, PAD)
        for pair in range(HEADS // 2):
            at = pair * 2 * HEAD_DIM
            q = packed_ref[here, at : at + 128]
            k = packed_ref[here, D + at : D + at + 128]
            v = packed_ref[here, 2 * D + at : 2 * D + at + 128]
            do = do_ref[here, at : at + 128]
            dq = dk = dv = None
            for side in range(2):
                mine = (lane >= HEAD_DIM) == bool(side)
                own = lambda a: jnp.where(mine, a, jnp.zeros_like(a))
                q_own, k_own, do_own = own(q), own(k), own(do)
                chances = softmax_rows(q_own, k)
                dv_part = dot(chances.astype(BF16), do_own, 0, 0)
                da = dot(do_own, v, 1, 1)
                ds = chances * (da - jnp.sum(da * chances, axis=-1, keepdims=True))
                ds = ds.astype(BF16)
                dq_part = dot(ds, k_own)
                dk_part = dot(ds, q_own, 0, 0)
                dq = dq_part if dq is None else dq + dq_part
                dk = dk_part if dk is None else dk + dk_part
                dv = dv_part if dv is None else dv + dv_part
            dp_ref[here, at : at + 128] = (dq * factor).astype(BF16)
            dp_ref[here, D + at : D + at + 128] = (dk * factor).astype(BF16)
            dp_ref[here, 2 * D + at : 2 * D + at + 128] = dv.astype(BF16)
    wait_all(wi_copies)
    dn = dot(dp_ref[...], wi_held[...].reshape(D, 3 * D), 1, 1)
    unit, scale = unit_rows(x_ref[...].astype(F32))
    dx, dgain = norm_backward(unit, scale, gain, dn)
    dx_ref[...] = dz_ref[...] + dx
    dgain_ref[...] = dgain
    for target, place, shard in shards_of(pos_ref, send_ref, keep_ref):
        columns = pl.ds(pl.multiple_of(shard * 128, 128), 128)
        grad_in = dot(normed_ref[:, columns], dp_ref[...], 0, 0).astype(BF16)
        grad_out = dot(o_ref[:, columns], dout_ref[...], 0, 0).astype(BF16)
        for half in range(2):
            there = own_half(pos_ref, half)
            target[place, there, :, 0 : 3 * D] = grad_in[half * 64 : half * 64 + 64]
            target[place, there, :, 3 * D : 4 * D] = grad_out[half * 64 : half * 64 + 64]
    if smalls:
        small = jnp.concatenate([dgain] + [ref[...] for ref in extra], axis=0)
        small = jnp.concatenate([small, jnp.zeros((-small.shape[0] % STRIP, D), F32)], axis=0)
        for target, place, shard in shards_of(pos_ref, send_ref, keep_ref):
            piece = jnp.zeros((small.shape[0], 128), F32)
            for s in range(4):
                piece = jnp.where(shard == s, small[:, s * 128 : (s + 1) * 128], piece)
            piece = piece.astype(BF16)
            for half in range(2):
                for strip in range(64 // STRIP):
                    for group in range(small.shape[0] // STRIP):
                        at = 4 * D + group * 128
                        target[place, half, strip * STRIP : (strip + 1) * STRIP, at : at + 128] = piece[
                            group * STRIP : (group + 1) * STRIP
                        ]


def feed_forward_kernel(pos_ref, x_ref, gain_ref, *refs):
    w1, w2 = refs[0:4], refs[4:8]
    y_ref, w1_held, w2_held, sems = refs[8:]
    w1_copies = start_weight(pos_ref, w1, w1_held, sems, 0)
    w2_copies = start_weight(pos_ref, w2, w2_held, sems, 4)
    unit, _ = unit_rows(x_ref[...])
    normed = (unit * gain_ref[...]).astype(BF16)
    wait_all(w1_copies)
    total = x_ref[...]
    for j in range(FF // CHUNK):
        at = slice(j * CHUNK, (j + 1) * CHUNK)
        active = gelu(dot(normed, w1_held[:, :, at].reshape(D, CHUNK))).astype(BF16)
        if j == 0:
            wait_all(w2_copies)
        total = total + dot(active, w2_held[...].reshape(FF, D)[at])
    y_ref[...] = total


def feed_backward_kernel(pos_ref, x_ref, gain_ref, dz_ref, *refs):
    w1, w2 = refs[0:4], refs[4:8]
    dx_ref, dgain_ref, send_ref, keep_ref, w1_held, w2_held, g1_ref, g2_ref, sems = refs[8:]
    w1_copies = start_weight(pos_ref, w1, w1_held, sems, 0)
    w2_copies = start_weight(pos_ref, w2, w2_held, sems, 4)
    unit, scale = unit_rows(x_ref[...])
    gain = gain_ref[...]
    normed = (unit * gain).astype(BF16)
    dout = dz_ref[...].astype(BF16)
    wait_all(w1_copies)
    wait_all(w2_copies)
    dn = None
    for j in range(FF // CHUNK):
        at = slice(j * CHUNK, (j + 1) * CHUNK)
        w1_now = w1_held[:, :, at].reshape(D, CHUNK)
        w2_now = w2_held[...].reshape(FF, D)[at]
        active, slope = gelu_parts(dot(normed, w1_now))
        dh = (slope * dot(dout, w2_now, 1, 1)).astype(BF16)
        g2_ref[at] = dot(active.astype(BF16), dout, 0, 0).astype(BF16)
        g1_ref[:, at] = dot(normed, dh, 0, 0).astype(BF16)
        part = dot(dh, w1_now, 1, 1)
        dn = part if dn is None else dn + part
    dx, dgain = norm_backward(unit, scale, gain, dn)
    dx_ref[...] = dz_ref[...] + dx
    dgain_ref[...] = dgain
    for target, place, shard in shards_of(pos_ref, send_ref, keep_ref):
        for half in range(2):
            there = own_half(pos_ref, half)
            target[place, there, 0:64] = g1_ref[pl.ds(pl.multiple_of(shard * 128 + half * 64, 64), 64)]
            for part in range(4):
                start = pl.multiple_of(shard * 512 + part * 128 + half * 64, 64)
                target[place, there, 64:128, part * 512 : (part + 1) * 512] = g2_ref[pl.ds(start, 64)]


def routing_kernel(slots, ids_ref, cot_ref, index_ref, blocks_ref):
    experts = blocks_ref.shape[0] // slots
    tokens = ids_ref.shape[1]
    expert = lax.broadcasted_iota(jnp.int32, (experts, tokens), 0)
    named = [ids_ref[k : k + 1, :] == expert for k in range(TOP)]
    matches = jnp.where(named[0] | named[1], 1.0, 0.0).astype(BF16)
    earlier = lax.broadcasted_iota(jnp.int32, (tokens, tokens), 0) < lax.broadcasted_iota(
        jnp.int32, (tokens, tokens), 1
    )
    rank = dot(matches, jnp.where(earlier, 1.0, 0.0).astype(BF16))
    index_ref[...] = jnp.full(index_ref.shape, -1, jnp.int32)
    place = lax.broadcasted_iota(jnp.int32, (blocks_ref.shape[0], tokens), 0)
    chosen = None
    for k in range(TOP):
        slot = jnp.sum(jnp.where(named[k], rank, 0.0), axis=0, keepdims=True).astype(jnp.int32)
        index = ids_ref[k : k + 1, :] * slots + slot
        index_ref[k : k + 1, :] = index
        hit = place == index
        chosen = hit if chosen is None else chosen | hit
    blocks_ref[...] = dot(jnp.where(chosen, 1.0, 0.0).astype(BF16), cot_ref[...]).astype(BF16)


def write_spare(slots, column):
    eye = lax.broadcasted_iota(jnp.int32, (slots, D), 0) == lax.broadcasted_iota(jnp.int32, (slots, D), 1)
    line = jnp.sum(jnp.where(eye, column, 0.0), axis=0, keepdims=True)
    high = line.astype(BF16).astype(F32)
    middle = (line - high).astype(BF16).astype(F32)
    low = line - high - middle
    row = lax.broadcasted_iota(jnp.int32, (8, D), 0)
    return jnp.where(row == 0, high, jnp.where(row == 1, middle, jnp.where(row == 2, low, 0.0)))


def read_spare(tile, slots):
    line = tile[0:1] + tile[1:2] + tile[2:3]
    eye = lax.broadcasted_iota(jnp.int32, (slots, D), 0) == lax.broadcasted_iota(jnp.int32, (slots, D), 1)
    return jnp.sum(jnp.where(eye, line, 0.0), axis=1, keepdims=True)


def small_kernel(pos_ref, *refs):
    out_ref = refs[4]
    for j in range(4):
        start = pl.multiple_of((pos_ref[0] ^ j) * 128, 128)
        out_ref[:, pl.ds(start, 128)] = refs[j][...].astype(F32)


def dispatch_kernel(slots, pos_ref, x_ref, gain_ref, router_ref, ids_ref, index_ref, c_ref, gate_ref, *blocks):
    tokens = x_ref.shape[0]
    each = blocks[0].shape[0] // slots
    experts = len(blocks) * each
    unit, _ = unit_rows(x_ref[...])
    c = (unit * gain_ref[...]).astype(BF16)
    c_ref[...] = c
    logits = dot(router_ref[...].astype(BF16), c, 1, 1)
    expert = lax.broadcasted_iota(jnp.int32, (experts, tokens), 0)
    picked = [
        jnp.sum(jnp.where(ids_ref[k : k + 1, :] == expert, logits, 0.0), axis=0, keepdims=True) for k in range(TOP)
    ]
    gates = [0.5 + 0.5 * jnp.tanh(0.5 * (picked[k] - picked[1 - k])) for k in range(TOP)]
    gate_ref[...] = jnp.concatenate(gates + [jnp.zeros((8 - TOP, tokens), F32)], axis=0)
    for k in range(experts):
        place = lax.broadcasted_iota(jnp.int32, (slots, tokens), 0) + (pos_ref[1] ^ k) * slots
        hits = [place == index_ref[k : k + 1, :] for k in range(TOP)]
        rows = dot(jnp.where(hits[0] | hits[1], 1.0, 0.0).astype(BF16), c)
        weight = sum(jnp.where(hits[k], gates[k], 0.0) for k in range(TOP))
        tile = write_spare(slots, jnp.sum(weight, axis=1, keepdims=True))
        at = k % each * slots
        blocks[k // each][at : at + slots] = jnp.concatenate([rows[: slots - 8], tile], axis=0).astype(BF16)


def experts_kernel(slots, n, each, pos_ref, w1_ref, w2_ref, *refs):
    g_refs, c_refs, refs = refs[: n * each], refs[n * each : n * each + n], refs[n * each + n :]
    dc_refs, z_refs = refs[:n], refs[n : 2 * n]
    f_ref, dh_ref, dy_ref, gate_ref, y_ref, dc_ref = refs[2 * n :]
    step = pl.program_id(0)
    blocks = [(b, slice(b * slots, (b + 1) * slots)) for b in range(n * each)]

    @pl.when(step == 0)
    def _():
        for b, here in blocks:
            end = (b % each + 1) * slots
            gate = read_spare(c_refs[b // each][end - 8 : end].astype(F32), slots)
            gate_ref[here] = jnp.broadcast_to(gate, (slots, 128))
            dy_ref[here] = (gate * g_refs[b][0].astype(F32)).astype(BF16)

    c = c_refs[0][...] if n == 1 else jnp.concatenate([ref[...] for ref in c_refs], axis=0)
    active, slope = gelu_parts(dot(c, w1_ref[...]))
    active = active.astype(BF16)
    f_ref[...] = active
    dh = (slope * dot(dy_ref[...], w2_ref[...], 1, 1)).astype(BF16)
    dh_ref[...] = dh
    y = dot(active, w2_ref[...])
    dc = dot(dh, w1_ref[...], 1, 1)

    @pl.when(step == 0)
    def _():
        y_ref[...] = y
        dc_ref[...] = dc

    @pl.when(step > 0)
    def _():
        y_ref[...] += y
        dc_ref[...] += dc

    @pl.when(step == pl.num_programs(0) - 1)
    def _():
        for b, here in blocks:
            there = slice(b % each * slots, (b % each + 1) * slots)
            rounded = y_ref[here].astype(BF16).astype(F32)
            dgate = jnp.sum(g_refs[b][0].astype(F32) * rounded, axis=1, keepdims=True)
            z_refs[b // each][there] = (gate_ref[here, 0:1] * rounded).astype(BF16)
            rows = jnp.concatenate([dc_ref[here][: slots - 8], write_spare(slots, dgate)], axis=0)
            dc_refs[b // each][there] = rows.astype(BF16)


def expert_grads_kernel(n, pos_ref, *refs):
    m = len(refs) - 2 - 3 * n
    c_refs = refs[:m]
    f_refs, dh_refs, dy_refs = refs[m : m + n], refs[m + n : m + 2 * n], refs[m + 2 * n : m + 3 * n]
    send_ref, keep_ref = refs[m + 3 * n :]
    per = m // n
    for target, half in ((send_ref, 1 - (pos_ref[0] & 1)), (keep_ref, pos_ref[0] & 1)):
        at = pl.ds(pl.multiple_of(half * 256, 256), 256)
        total1 = total2 = None
        for i in range(n):
            c = [ref[:, at] for ref in c_refs[i * per : (i + 1) * per]]
            c = c[0] if per == 1 else jnp.concatenate(c, axis=0)
            part1 = dot(c, dh_refs[i][...], 0, 0)
            part2 = dot(f_refs[i][...], dy_refs[i][:, at], 0, 0)
            total1 = part1 if total1 is None else total1 + part1
            total2 = part2 if total2 is None else total2 + part2
        target[0:256] = total1.astype(BF16)
        target[256:512, 0:256] = total2[0:256].astype(BF16)
        target[256:512, 256:512] = total2[256:512].astype(BF16)


def cut_kernel(a_ref, b_ref, *outs):
    row = 0
    for out in outs:
        rows = slice(row, row + out.shape[0])
        out[...] = (a_ref[rows].astype(F32) + b_ref[rows].astype(F32)).astype(BF16)
        row += out.shape[0]


def glue_kernel(*refs):
    n, row = (len(refs) - 1) // 2, 0
    for a_ref, b_ref in zip(refs[:n], refs[n : 2 * n]):
        refs[-1][row : row + a_ref.shape[0]] = (a_ref[...].astype(F32) + b_ref[...].astype(F32)).astype(BF16)
        row += a_ref.shape[0]


def join_kernel(pos_ref, own_ref, other_ref, out1_ref, out2_ref):
    core = pos_ref[0] & 1
    for mine, ref in ((core, own_ref), (1 - core, other_ref)):
        at = pl.ds(pl.multiple_of(mine * 256, 256), 256)
        out1_ref[at] = ref[0:256].astype(F32)
        for block in range(FF // 256):
            out2_ref[block * 256 : (block + 1) * 256, at] = ref[256:512, block * 256 : (block + 1) * 256].astype(F32)


def arrange_kernel(pos_ref, *refs):
    for k, ref in enumerate(refs[:-1]):
        refs[-1][pos_ref[1] ^ k] = ref[...]


def one_hot_columns(index_ref, width):
    place = lax.broadcasted_iota(jnp.int32, (index_ref.shape[0], width), 1)
    hit = (place == index_ref[:, 0:1]) | (place == index_ref[:, 1:2])
    return jnp.where(hit, 1.0, 0.0).astype(BF16)


def combine_kernel(
    slots, pos_ref, x_ref, gain_ref, router_ref, ids_ref, index_ref, turned_ref, c_ref, gate_ref, cot_ref, *refs
):
    blocks, (dx_ref, dgain_ref, drouter_ref) = refs[:-3], refs[-3:]
    each = blocks[0].shape[0] // slots
    experts = len(blocks) * each
    tokens = x_ref.shape[0]
    dgates = [jnp.zeros((1, tokens), F32) for _ in range(TOP)]
    gc = None
    for k in range(experts):
        at = k % each * slots
        block = blocks[k // each][at : at + slots]
        start = (pos_ref[1] ^ k) * slots
        place = lax.broadcasted_iota(jnp.int32, (tokens, slots), 1) + start
        hit = (place == turned_ref[:, 0:1]) | (place == turned_ref[:, 1:2])
        part = dot(jnp.where(hit, 1.0, 0.0).astype(BF16), block)
        gc = part if gc is None else gc + part
        place = lax.broadcasted_iota(jnp.int32, (slots, tokens), 0) + start
        column = read_spare(block[slots - 8 :].astype(F32), slots)
        for j in range(TOP):
            hit = place == index_ref[j : j + 1, :]
            dgates[j] = dgates[j] + jnp.sum(jnp.where(hit, column, 0.0), axis=0, keepdims=True)
    dl = gate_ref[0:1] * gate_ref[1:2] * (dgates[0] - dgates[1])
    expert = lax.broadcasted_iota(jnp.int32, (experts, tokens), 0)
    dlogits = jnp.where(ids_ref[0:1, :] == expert, dl, 0.0) - jnp.where(ids_ref[1:2, :] == expert, dl, 0.0)
    dlogits = dlogits.astype(BF16)
    gc = gc + dot(dlogits, router_ref[...].astype(BF16), 0, 0)
    drouter_ref[...] = dot(dlogits, c_ref[...])
    unit, scale = unit_rows(x_ref[...])
    dx, dgain = norm_backward(unit, scale, gain_ref[...], gc)
    dx_ref[...] = cot_ref[...].astype(F32) + dx
    dgain_ref[...] = dgain


def split_cube_kernel(n, pos_ref, *refs):
    kept, came, out_ref = refs[0:n], refs[n : 2 * n], refs[2 * n]
    for place in range(2):
        for half in range(2):
            x = (pos_ref[1] & 1) ^ (1 - half)
            y = (pos_ref[0] >> 1) ^ (1 - place)
            row = 0
            for keep, new in zip(kept, came):
                total = (keep[place, half].astype(F32) + new[place, half].astype(F32)).astype(BF16)
                for start in range(0, keep.shape[2], 64):
                    for depth in range(2):
                        at = start + depth * STRIP
                        out_ref[depth * 4 + x * 2 + y, row : row + STRIP] = total[at : at + STRIP]
                    row += STRIP


def sum_cube_kernel(a_ref, out_ref):
    total = a_ref[0].astype(F32)
    for k in range(1, a_ref.shape[0]):
        total = total + a_ref[k].astype(F32)
    out_ref[...] = total.astype(BF16)


def sum_kernel(*refs):
    total = refs[0][...].astype(F32)
    for ref in refs[1:-1]:
        total = total + ref[...].astype(F32)
    refs[-1][...] = total.astype(BF16)


def rows_of(pos_ref, k):
    source = pos_ref[1] ^ k
    return pl.ds(pl.multiple_of((source & 1) * 64 + (source >> 1 & 1) * STRIP, STRIP), STRIP)


def finish_mlp_kernel(pos_ref, *refs):
    mlp1_ref, mlp2_ref = refs[4:]
    for k in range(4):
        there = rows_of(pos_ref, k)
        mlp1_ref[there] = refs[k][STRIP : 2 * STRIP].astype(F32)
        for part in range(4):
            mlp2_ref[part, there] = refs[k][2 * STRIP :, part * 512 : (part + 1) * 512].astype(F32)


def finish_attention_kernel(pos_ref, *refs):
    in_ref, out_ref, small_ref = refs[8:]
    for k in range(4):
        there = rows_of(pos_ref, k)
        for layer, ref in ((0, refs[k]), (1, refs[4 + k])):
            in_ref[layer, there] = ref[0:STRIP, 0 : 3 * D].astype(F32)
            out_ref[layer, there] = ref[0:STRIP, 3 * D : 4 * D].astype(F32)
    for group in range(small_ref.shape[0] // STRIP):
        at = 4 * D + group * 128
        small_ref[group * STRIP : (group + 1) * STRIP] = refs[0][:, at : at + 128].astype(F32)


def final_kernel(blocks_ref, x_ref, turned_ref, out_ref):
    out_ref[...] = (x_ref[...] + dot(one_hot_columns(turned_ref, blocks_ref.shape[0]), blocks_ref[...])).astype(BF16)


def spent(us):
    return pl.CostEstimate(flops=int(us * 1.0e9), bytes_accessed=0, transcendentals=0)


def call(kernel, outs, *args, us=1.0, scratch=(), specs=None, room=40, **more):
    return list(
        pl.pallas_call(
        kernel,
        out_shape=[(pltpu.HBM if rest else jax.ShapeDtypeStruct)(shape, kind) for shape, kind, *rest in outs],
        in_specs=specs if specs is not None else [WHOLE] * len(args),
        out_specs=[WHOLE] * len(outs),
        scratch_shapes=list(scratch),
        cost_estimate=spent(us),
        compiler_params=pltpu.CompilerParams(vmem_limit_bytes=room * 1024 * 1024),
        **more,
        )(*args)
    )


WHOLE = pl.BlockSpec(memory_space=pltpu.VMEM)
SCALAR = pl.BlockSpec(memory_space=pltpu.SMEM)
AWAY = pl.BlockSpec(memory_space=pltpu.HBM)


def flip(array, axis, bit):
    return lax.ppermute(array, axis, [(i, i ^ bit) for i in range(lax.axis_size(axis))])


def gather_pieces(piece, across=None):
    across = flip(piece, "wshard", 2) if across is None else across
    return (piece, flip(piece, "wshard", 1), across, flip(across, "wshard", 1))


def after(array, *others):
    return lax.optimization_barrier((array, *others))[0]


def split_cube(pos, bundle):
    came = [flip(send, "wshard", 1) for send, _ in bundle]
    tall = sum(keep.shape[2] for _, keep in bundle)
    wide = bundle[0][0].shape[-1]
    return call(
        functools.partial(split_cube_kernel, len(bundle)),
        [((8, tall // 2, wide), BF16, AWAY)],
        pos,
        *[keep for _, keep in bundle],
        *came,
        specs=[SCALAR] + [WHOLE] * (2 * len(bundle)),
        us=3.0,
    )[0]


def trade_cube(blocks):
    inner = lax.axis_size("wshard")
    groups = [
        [((2 * z + depth) * 2 + x) * inner + y * 2 + core for depth in range(2) for x in range(2) for y in range(2)]
        for z in range(lax.axis_size("expert") // 4)
        for core in range(2)
    ]
    return lax.all_to_all(blocks, ("expert", "wshard"), 0, 0, axis_index_groups=groups, tiled=True)


def sum_cube(blocks):
    return call(sum_cube_kernel, [(blocks.shape[1:], BF16, AWAY)], blocks, us=2.0)[0]


def sum_two(strip, other):
    return call(sum_kernel, [(strip.shape, BF16, AWAY)], strip, other)[0]


def spread(strip):
    return [strip] + [flip(strip, "expert", k) for k in range(1, 4)]


def sum_plainly(send, keep):
    half = (keep.astype(F32) + flip(send, "wshard", 1).astype(F32)).astype(BF16)
    rows = half[1].astype(F32) + flip(half[0], "wshard", 2).astype(F32)
    return lax.psum(jnp.concatenate([rows[1], rows[0]], axis=0), "expert")


def expand(rows, images):
    return jnp.pad(rows.reshape(images, SEQ, -1), ((0, 0), (0, PAD - SEQ), (0, 0))).reshape(images * PAD, -1)


def contract(rows, images):
    return rows.reshape(images, PAD, -1)[:, :SEQ].reshape(images * SEQ, -1)


def local(
    images, attn_in, attn_out, norm_gains, mlp_in, mlp_out, router, expert_in, expert_out, expert_ids, cotangent
):
    owners = lax.axis_size("expert")
    experts = owners * expert_in.shape[0]
    tokens = images.shape[0]
    pictures = tokens // SEQ
    rows = pictures * PAD
    capacity = max(2, 2 * TOP * tokens // experts)
    slots = (capacity + 8 + 15) // 16 * 16
    every = experts * slots
    linked = owners == LINKED
    own = lax.axis_index("expert") if linked else 0
    pos = jnp.stack([lax.axis_index("wshard"), own]).astype(jnp.int32)

    small = jnp.concatenate([norm_gains, router.T], axis=0)
    small = jnp.pad(small, ((0, -small.shape[0] % 16), (0, 0)))
    (small_full,) = call(
        small_kernel, [((small.shape[0], D), F32)], pos, *gather_pieces(small), specs=[SCALAR] + [WHOLE] * 4
    )
    gains = [small_full[i : i + 1] for i in range(4)]
    router_full = small_full[4 : 4 + experts]

    wi0 = flip(attn_in[0], "wshard", 2)
    wo0 = flip(attn_out[0], "wshard", 2)
    w1_across = flip(after(mlp_in, wi0), "wshard", 2)
    w2_across = flip(after(mlp_out, wi0), "wshard", 2)
    wi1 = flip(after(attn_in[1], w1_across), "wshard", 2)
    wo1 = flip(after(attn_out[1], w1_across), "wshard", 2)
    wi = [gather_pieces(attn_in[0], wi0), None]
    wo = [gather_pieces(attn_out[0], wo0), None]
    x0 = expand(images, pictures)

    weight_specs = [AWAY] * 8
    attn_scratch = [pltpu.VMEM((4, D // 4, 3 * D), BF16), pltpu.VMEM((4, D // 4, D), BF16)]
    mlp_scratch = [pltpu.VMEM((4, D // 4, FF), BF16), pltpu.VMEM((4, FF // 4, D), BF16)]
    sems = pltpu.SemaphoreType.DMA((8,))

    def attend(x, layer):
        return call(
            attend_forward_kernel,
            [((rows, D), F32), ((rows, 3 * D), BF16), ((rows, D), BF16)],
            pos, x, gains[2 * layer], *wi[layer], *wo[layer],
            specs=[SCALAR, WHOLE, WHOLE] + weight_specs,
            scratch=attn_scratch + [sems],
            us=7.0,
        )

    def attend_back(x, layer, packed, o, dz, extra):
        wide = 4 * D
        if extra:
            wide += (sum(a.shape[0] for a in extra) + 1 + STRIP - 1) // STRIP * 128
        return call(
            functools.partial(attend_backward_kernel, len(extra)),
            [((rows, D), F32), ((1, D), F32), ((2, 2, 64, wide), BF16, AWAY), ((2, 2, 64, wide), BF16, AWAY)],
            pos, x, gains[2 * layer], packed, o, dz, *wi[layer], *wo[layer], *extra,
            specs=[SCALAR] + [WHOLE] * 5 + weight_specs + [WHOLE] * len(extra),
            scratch=attn_scratch
            + [pltpu.VMEM((rows, 3 * D), BF16)]
            + [pltpu.VMEM((rows, D), BF16)] * 3
            + [sems],
            us=12.5,
            room=58,
        )

    x1, packed1, o1 = attend(x0, 0)
    ids = jnp.pad(after(expert_ids, x1).T.reshape(TOP, pictures, SEQ), ((0, 8 - TOP), (0, 0), (0, PAD - SEQ)), constant_values=-1)
    ids = ids.reshape(8, rows)
    cot = expand(after(cotangent, x1), pictures)

    index, g_out = call(
        functools.partial(routing_kernel, slots), [((8, rows), jnp.int32), ((every, D), BF16)], ids, cot, us=3.4
    )
    turned = index.T
    trade = functools.partial(lax.all_to_all, axis_name="expert", split_axis=0, concat_axis=0, tiled=True)
    g_in = trade(g_out.reshape(experts, slots, D))

    w1 = gather_pieces(mlp_in, after(w1_across, x1))
    w2 = gather_pieces(mlp_out, after(w2_across, x1))
    (x2,) = call(
        feed_forward_kernel, [((rows, D), F32)], pos, x1, gains[1], *w1, *w2,
        specs=[SCALAR, WHOLE, WHOLE] + weight_specs, scratch=mlp_scratch + [sems], us=6.5,
    )
    wi[1] = gather_pieces(attn_in[1], after(wi1, x2))
    wo[1] = gather_pieces(attn_out[1], after(wo1, x2))
    x3, packed2, o2 = attend(x2, 1)
    arrays = experts if linked else max(1, experts // (2 * PAD // slots))
    each = experts // arrays
    c, gate, *c_out = call(
        functools.partial(dispatch_kernel, slots),
        [((rows, D), BF16), ((8, rows), F32)] + [((each * slots, D), BF16, AWAY)] * arrays,
        pos, x3, gains[3], router_full, ids, index,
        specs=[SCALAR] + [WHOLE] * 5,
        us=4.6,
    )

    def swap(blocks, first=0):
        if linked:
            return [flip(block, "expert", k) if k else block for k, block in enumerate(blocks, first)]
        moved = trade(jnp.concatenate(blocks).reshape(experts, slots, D))
        return list(moved.reshape(arrays, each * slots, D))

    c_in = swap(c_out)
    per = 2 if linked else 1
    work = []
    dc_out, z_out, dc_in = [], [], []
    for first in range(0, arrays, per):
        given = c_in[first : first + per]
        if linked and first >= 2 * per:
            given[0], *dc_in[-2 * per : -per] = lax.optimization_barrier((given[0], *dc_in[-2 * per : -per]))
        count = list(range(first * each, (first + per) * each))
        tall = len(count) * slots
        fixed = lambda *shape: pl.BlockSpec(shape, lambda j, pos_ref: (0,) * len(shape))
        source = lambda k: pl.BlockSpec((1, slots, D), lambda j, pos_ref: (pos_ref[1] ^ k, 0, 0))
        across = lambda height: pl.BlockSpec((height, CHUNK), lambda j, pos_ref: (0, j))
        *made, f, dh, dy = pl.pallas_call(
            functools.partial(experts_kernel, slots, per, each),
            out_shape=[pltpu.HBM((each * slots, D), BF16)] * (2 * per)
            + [pltpu.HBM((tall, FF), BF16)] * 2
            + [pltpu.HBM((tall, D), BF16)],
            grid_spec=pltpu.PrefetchScalarGridSpec(
                num_scalar_prefetch=1,
                grid=(FF // CHUNK,),
                in_specs=[across(D), pl.BlockSpec((CHUNK, D), lambda j, pos_ref: (j, 0))]
                + [source(k) for k in count]
                + [fixed(each * slots, D)] * per,
                out_specs=[fixed(each * slots, D)] * (2 * per) + [across(tall)] * 2 + [fixed(tall, D)],
                scratch_shapes=[pltpu.VMEM((tall, 128), F32), pltpu.VMEM((tall, D), F32), pltpu.VMEM((tall, D), F32)],
            ),
            cost_estimate=spent(8.0),
            compiler_params=pltpu.CompilerParams(vmem_limit_bytes=VMEM_LIMIT),
        )(pos, expert_in[0], expert_out[0], *[g_in] * len(count), *given)
        dc_out += made[:per]
        z_out += made[per:]
        if linked:
            dc_in += swap(made[:per], first)
        work.append((f, dh, dy))
    if not linked:
        dc_in = swap(dc_out)
    if linked:
        (z_block,) = call(
            arrange_kernel, [((experts, slots, D), BF16, AWAY)], pos, *z_out, specs=[SCALAR] + [WHOLE] * experts, us=2.0
        )
    else:
        z_block = jnp.concatenate(z_out).reshape(experts, slots, D)
    n = len(work)
    whole_rows = lambda a: pl.BlockSpec(a.shape, lambda j: (0, 0))
    chunk = lambda a: pl.BlockSpec((a.shape[0], CHUNK), lambda j: (0, j))
    fs, dhs, dys = ([w[i] for w in work] for i in range(3))
    if linked:
        dys[0], *dc_in[per : 2 * per] = lax.optimization_barrier((dys[0], *dc_in[per : 2 * per]))
    grad_send, grad_keep = pl.pallas_call(
        functools.partial(expert_grads_kernel, n),
        grid=(FF // CHUNK,),
        in_specs=[SCALAR]
        + [whole_rows(a) for a in c_in]
        + [chunk(a) for a in fs + dhs]
        + [whole_rows(a) for a in dys],
        out_specs=[pl.BlockSpec((512, CHUNK), lambda j: (0, j))] * 2,
        out_shape=[pltpu.HBM((512, FF), BF16)] * 2,
        cost_estimate=spent(10.0),
        compiler_params=pltpu.CompilerParams(vmem_limit_bytes=VMEM_LIMIT),
    )(pos, *c_in, *fs, *dhs, *dys)
    x3_late, z_block, grad_send, grad_keep = lax.optimization_barrier((x3, z_block, grad_send, grad_keep))
    g3, gain3, drouter = call(
        functools.partial(combine_kernel, slots),
        [((rows, D), F32), ((1, D), F32), ((experts, D), F32)],
        pos, x3_late, gains[3], router_full, ids, index, turned, c, gate, cot, *dc_in,
        specs=[SCALAR] + [WHOLE] * (9 + arrays),
        us=5.5,
    )
    g3, z_block, grad_send = lax.optimization_barrier((g3, z_block, grad_send))
    z_in = trade(z_block)
    grads = call(
        cut_kernel,
        [((tall, FF), BF16, AWAY) for tall in (128, 128, 256)],
        grad_keep, flip(grad_send, "wshard", 1),
        us=2.0,
    )
    g3 = after(g3, *grads)
    crossed = [flip(piece, "wshard", 2) for piece in grads[:2]]
    g2, gain2, *second = attend_back(x2, 1, packed2, o2, g3, [])
    g1, gain1, *mlp = call(
        feed_backward_kernel,
        [((rows, D), F32), ((1, D), F32)] + [((2, 2, 128, FF), BF16, AWAY)] * 2,
        pos, x1, gains[1], g2, *w1, *w2,
        specs=[SCALAR, WHOLE, WHOLE, WHOLE] + weight_specs,
        scratch=mlp_scratch + [pltpu.VMEM((D, FF), BF16), pltpu.VMEM((FF, D), BF16), sems],
        us=12.5,
        room=58,
    )
    *second, mlp[0], mlp[1], crossed[0], crossed[1] = lax.optimization_barrier(
        (*second, mlp[0], mlp[1], crossed[0], crossed[1])
    )
    if linked:
        bulk = split_cube(pos, [second, mlp])
        g1 = after(g1, z_in, bulk)
        bulk = trade_cube(bulk)
    dx, _, *first = attend_back(x0, 0, packed1, o1, g1, [gain1, gain2, gain3, drouter])
    (final,) = call(final_kernel, [((rows, D), BF16)], z_in.reshape(every, D), x3, turned, us=3.5)

    wide = first[0].shape[-1]
    if linked:
        tail = split_cube(pos, [(first[0], after(first[1], final))])
        final_rows, input_grad = contract(final, pictures), contract(dx, pictures)
        bulk = sum_cube(after(bulk, tail, final_rows, input_grad))
        deep = flip(bulk, "expert", 4)
        tail = sum_cube(after(trade_cube(after(tail, bulk)), deep))
        last = flip(after(grads[2], tail), "wshard", 2)
        bulk = spread(sum_two(bulk, deep))
        tail = sum_two(tail, flip(tail, "expert", 4))
        crossed.append(after(last, tail, *bulk))
        tail = spread(tail)
        mlp1, mlp2 = call(
            finish_mlp_kernel,
            [((D // 4, FF), F32), ((4, 128, D), F32)],
            pos, *bulk, specs=[SCALAR] + [WHOLE] * 4, us=2.0,
        )
        grad_in, grad_out, smalls = call(
            finish_attention_kernel,
            [((2, D // 4, 3 * D), F32), ((2, D // 4, D), F32), (((wide - 4 * D) // 128 * STRIP, 128), F32)],
            pos, *tail, *bulk, specs=[SCALAR] + [WHOLE] * 8, us=2.0,
        )
        mlp2 = mlp2.reshape(FF // 4, D)
    else:
        first, second, mlp = sum_plainly(*first), sum_plainly(*second), sum_plainly(*mlp)
        grad_in = jnp.stack([first[:, : 3 * D], second[:, : 3 * D]])
        grad_out = jnp.stack([first[:, 3 * D : 4 * D], second[:, 3 * D :]])
        smalls = first[:STRIP, 4 * D :].reshape(STRIP, -1, 128).transpose(1, 0, 2).reshape(-1, 128)
        mlp1 = jnp.concatenate([mlp[0:64], mlp[128:192]], axis=0)
        final_rows, input_grad = contract(final, pictures), contract(dx, pictures)
        mlp2 = jnp.stack([mlp[64:128], mlp[192:256]]).reshape(2, 64, 4, D).transpose(2, 0, 1, 3).reshape(FF // 4, D)

    if not linked:
        crossed.append(flip(grads[2], "wshard", 2))
    (joined,) = call(glue_kernel, [((512, FF), BF16, AWAY)], *grads, *crossed, us=2.0)
    expert1, expert2 = call(
        join_kernel,
        [((D, FF), F32), ((FF, D), F32)],
        pos, joined, flip(joined, "wshard", 1),
        specs=[SCALAR] + [WHOLE] * 2,
        us=4.0,
    )

    return (
        final_rows,
        input_grad,
        grad_in,
        grad_out,
        smalls[0:4],
        mlp1,
        mlp2,
        smalls[4 : 4 + experts].T,
        expert1[None],
        expert2[None],
    )


def solution(mesh):
    rows = P(("expert", "wshard"), None)
    dense = (P(None, "wshard", None), P(None, "wshard", None), P(None, "wshard"))
    shards = (P("wshard", None),) * 3
    experts = (P("expert", None, None),) * 2
    return jax.shard_map(
        local,
        mesh=mesh,
        in_specs=(rows, *dense, *shards, *experts, rows, rows),
        out_specs=(rows, rows, *dense, *shards, *experts),
        check_vma=False,
    )
```

profile of v0, /device:TPU:0, one launch (start us, length us, event | category | flops | bytes accessed | tf_op | source)
XLA Modules:
  0.0 339.2 jit_solution(4077603805430255261)
XLA Ops:
  8.0 7.0 %collective-permute-done.1.refs_2_ = bf16[16,128]{1,0:T(8,128)(2,1)S(1)} collective-permute-done((bf16[16,128]{1,0:T(8,128)(2,1)S(1)}, bf16[16,128]{1,0:T(8,128)(2,1)S(1)}, u32[]{:S(2)}, u32[]{:S(2)}) %collective-permute-start.1) | collective-permute-done | bytes 4128 | tf_op jit(solution)/shard_map/ppermute | solution.py:536
  19.3 5.6 %shard_map.187 = (f32[416,512]{1,0:T(8,128)S(1)}, bf16[416,1536]{1,0:T(8,128)(2,1)S(1)}, bf16[416,512]{1,0:T(8,128)(2,1)S(1)}) custom-call(s32[2]{0:T(128)S(1)} %pad_add_fusion.pos_ref, bf16[416,512]{1,0:T(8,128)(2,1)S(1)} %bitcast.27, f32[1,512]{1,0:T(1,128)S(1)} %get-tuple-element.241.gain_ref, bf16[128,1536]{1,0:T(8,128)(2,1)S(1)} %get-tuple-element.235.refs_0_, ...), custom_call_target="tpu_custom_call" | custom-call | flops 7000000000 | tf_op jit(solution)/shard_map/pallas_call | solution.py:517
  31.5 6.8 %all-to-all-start = ((bf16[8,208,512]{2,1,0:T(8,128)(2,1)}), bf16[8,208,512]{2,1,0:T(8,128)(2,1)S(1)}, u32[]{:S(2)}, u32[]{:S(2)}) async-start(bf16[8,208,512]{2,1,0:T(8,128)(2,1)} %bitcast.12), calls=%async_computation | async-start | bytes 3407872 | tf_op jit(solution)/shard_map/all_to_all | solution.py:674
  38.9 4.0 %collective-permute-done.13.refs_6_ = bf16[512,512]{1,0:T(8,128)(2,1)} collective-permute-done((bf16[512,512]{1,0:T(8,128)(2,1)}, bf16[512,512]{1,0:T(8,128)(2,1)}, u32[]{:S(2)}, u32[]{:S(2)}) %collective-permute-start.13) | collective-permute-done | bytes 524320 | tf_op jit(solution)/shard_map/ppermute | solution.py:536
  46.9 4.4 %shard_map.188.x_ref = f32[416,512]{1,0:T(8,128)S(1)} custom-call(s32[2]{0:T(128)S(1)} %pad_add_fusion.pos_ref, f32[416,512]{1,0:T(8,128)S(1)} %copy-done.68, f32[1,512]{1,0:T(1,128)S(1)} %get-tuple-element.240.gain_ref, bf16[128,2048]{1,0:T(8,128)(2,1)S(1)} %copy-done.15, bf16[128,2048]{1,0:T(8,128)(2,1)S(1)} %collective-permute-done.9.refs_1_, ...), custom_call_target="tpu_custom_call" | custom-call | flops 6499999744 | tf_op jit(solution)/shard_map/pallas_call | solution.py:517
  56.5 3.9 %collective-permute-done.19.refs_6_ = bf16[128,512]{1,0:T(8,128)(2,1)S(1)} collective-permute-done((bf16[128,512]{1,0:T(8,128)(2,1)S(1)}, bf16[128,512]{1,0:T(8,128)(2,1)S(1)}, u32[]{:S(2)}, u32[]{:S(2)}) %collective-permute-start.19) | collective-permute-done | bytes 131104 | tf_op jit(solution)/shard_map/ppermute | solution.py:536
  61.8 5.6 %shard_map.189 = (f32[416,512]{1,0:T(8,128)S(1)}, bf16[416,1536]{1,0:T(8,128)(2,1)S(1)}, bf16[416,512]{1,0:T(8,128)(2,1)S(1)}) custom-call(s32[2]{0:T(128)S(1)} %pad_add_fusion.pos_ref, f32[416,512]{1,0:T(8,128)S(1)} %shard_map.188.x_ref, f32[1,512]{1,0:T(1,128)S(1)} %get-tuple-element.239.gain_ref, bf16[128,1536]{1,0:T(8,128)(2,1)S(1)} %get-tuple-element.127.refs_0_, ...), custom_call_target="tpu_custom_call" | custom-call | flops 7000000000 | tf_op jit(solution)/shard_map/pallas_call | solution.py:517
  88.7 8.6 %shard_map.192 = (bf16[208,512]{1,0:T(8,128)(2,1)}, bf16[208,512]{1,0:T(8,128)(2,1)}, bf16[208,512]{1,0:T(8,128)(2,1)}, bf16[208,512]{1,0:T(8,128)(2,1)}, bf16[4...) custom-call(s32[2]{0:T(128)S(1)} %pad_add_fusion.pos_ref, ...), custom_call_target="tpu_custom_call" | custom-call | flops 8000000000 | tf_op jit(solution)/shard_map/pallas_call | solution.py:714
  99.1 8.8 %shard_map.193 = (bf16[208,512]{1,0:T(8,128)(2,1)}, bf16[208,512]{1,0:T(8,128)(2,1)}, bf16[208,512]{1,0:T(8,128)(2,1)}, bf16[208,512]{1,0:T(8,128)(2,1)}, bf16[4...) custom-call(s32[2]{0:T(128)S(1)} %pad_add_fusion.pos_ref, ...), custom_call_target="tpu_custom_call" | custom-call | flops 8000000000 | tf_op jit(solution)/shard_map/pallas_call | solution.py:714
  110.9 9.7 %shard_map.194 = (bf16[208,512]{1,0:T(8,128)(2,1)}, bf16[208,512]{1,0:T(8,128)(2,1)}, bf16[208,512]{1,0:T(8,128)(2,1)}, bf16[208,512]{1,0:T(8,128)(2,1)}, bf16[4...) custom-call(s32[2]{0:T(128)S(1)} %pad_add_fusion.pos_ref, ...), custom_call_target="tpu_custom_call" | custom-call | flops 8000000000 | tf_op jit(solution)/shard_map/pallas_call | solution.py:714
  120.6 5.1 %collective-permute-start.31 = (bf16[208,512]{1,0:T(8,128)(2,1)}, bf16[208,512]{1,0:T(8,128)(2,1)S(1)}, u32[]{:S(2)}, u32[]{:S(2)}) collective-permute-start(bf16[208,512]{1,0:T(8,128)(2,1)} %get-tuple-element.182), channel_id=1, source_target_pairs={{0,16},{4,20},{8,24},{12,28},{16,0},{20,4},{24,8},{28,12},{1,17},{... | collective-permute-start | bytes 638984 | tf_op jit(solution)/shard_map/ppermute | solution.py:536
  127.1 10.3 %shard_map.195 = (bf16[208,512]{1,0:T(8,128)(2,1)}, bf16[208,512]{1,0:T(8,128)(2,1)}, bf16[208,512]{1,0:T(8,128)(2,1)}, bf16[208,512]{1,0:T(8,128)(2,1)}, bf16[4...) custom-call(s32[2]{0:T(128)S(1)} %pad_add_fusion.pos_ref, ...), custom_call_target="tpu_custom_call" | custom-call | flops 8000000000 | tf_op jit(solution)/shard_map/pallas_call | solution.py:714
  143.5 13.0 %shard_map.197 = (bf16[512,2048]{1,0:T(8,128)(2,1)}, bf16[512,2048]{1,0:T(8,128)(2,1)}) custom-call(s32[2]{0:T(128)S(1)} %pad_add_fusion.pos_ref, bf16[208,512]{1,0:T(8,128)(2,1)S(1)} %copy-done.79, bf16[208,512]{1,0:T(8,128)(2,1)S(1)} %collective-permute-done.21.refs_3_.refs_1_, bf16[208,512]{1,0:T(8,128)(2,1)S(1)} %collective-permute-done.22.refs_2_, ...), custom_call_target="tpu_custom_call" | custom-call | flops 10000000000 | tf_op jit(solution)/shard_map/pallas_call | solution.py:750
  163.6 7.8 %all-to-all-start.1 = ((bf16[8,208,512]{2,1,0:T(8,128)(2,1)}), bf16[8,208,512]{2,1,0:T(8,128)(2,1)S(1)}, u32[]{:S(2)}, u32[]{:S(2)}) async-start(bf16[8,208,512]{2,1,0:T(8,128)(2,1)} %shard_map.196), calls=%async_computation.1 | async-start | bytes 3407872 | tf_op jit(solution)/shard_map/all_to_all | solution.py:771
  178.3 12.5 %shard_map.201 = (f32[416,512]{1,0:T(8,128)}, f32[1,512]{1,0:T(1,128)}, bf16[2,2,64,2048]{3,2,1,0:T(8,128)(2,1)}, bf16[2,2,64,2048]{3,2,1,0:T(8,128)(2,1)}) custom-call(s32[2]{0:T(128)} %copy-done.42, f32[416,512]{1,0:T(8,128)} %copy-done.69, f32[1,512]{1,0:T(1,128)} %copy-done.9, bf16[416,1536]{1,0:T(8,128)(2,1)} %copy-done.70, ...), custom_call_target="tpu_custom_call" | custom-call | flops 12499999744 | tf_op jit(solution)/shard_map/pallas_call | solution.py:517
  190.8 13.0 %shard_map.202 = (f32[416,512]{1,0:T(8,128)}, f32[1,512]{1,0:T(1,128)}, bf16[2,2,128,2048]{3,2,1,0:T(8,128)(2,1)}, bf16[2,2,128,2048]{3,2,1,0:T(8,128)(2,1)}) custom-call(s32[2]{0:T(128)} %copy-done.42, f32[416,512]{1,0:T(8,128)} %copy-done.67, f32[1,512]{1,0:T(1,128)} %copy-done.8, f32[416,512]{1,0:T(8,128)} %get-tuple-element.201.dz_ref, ...), custom_call_target="tpu_custom_call" | custom-call | flops 12499999744 | tf_op jit(solution)/shard_map/pallas_call | solution.py:517
  206.0 4.8 %collective-permute-done.38.refs_2_ = bf16[2,2,64,2048]{3,2,1,0:T(8,128)(2,1)S(1)} collective-permute-done((bf16[2,2,64,2048]{3,2,1,0:T(8,128)(2,1)S(1)}, bf16[2,2,64,2048]{3,2,1,0:T(8,128)(2,1)S(1)}, u32[]{:S(2)}, u32[]{:S(2)}) %collective-permute-start.38) | collective-permute-done | bytes 1048608 | tf_op jit(solution)/shard_map/ppermute | solution.py:536
  217.0 5.2 %all-to-all-start.2 = ((bf16[8,96,2048]{2,1,0:T(8,128)(2,1)}), bf16[8,96,2048]{2,1,0:T(8,128)(2,1)S(1)}, u32[]{:S(2)}, u32[]{:S(2)}) async-start(bf16[8,96,2048]{2,1,0:T(8,128)(2,1)} %shard_map.203), calls=%async_computation.2 | async-start | bytes 6291456 | tf_op jit(solution)/shard_map/all_to_all | solution.py:570
  222.2 12.8 %shard_map.204 = (f32[416,512]{1,0:T(8,128)}, f32[1,512]{1,0:T(1,128)}, bf16[2,2,64,2176]{3,2,1,0:T(8,128)(2,1)}, bf16[2,2,64,2176]{3,2,1,0:T(8,128)(2,1)}) custom-call(s32[2]{0:T(128)} %copy-done.42, bf16[416,512]{1,0:T(8,128)(2,1)} %bitcast.28, f32[1,512]{1,0:T(1,128)} %copy-done.7, bf16[416,1536]{1,0:T(8,128)(2,1)} %copy-done.71, ...), custom_call_target="tpu_custom_call" | custom-call | flops 12499999744 | tf_op jit(solution)/shard_map/pallas_call | solution.py:517
  248.0 15.8 %all-to-all-done.2.a_ref = bf16[8,96,2048]{2,1,0:T(8,128)(2,1)S(1)} async-done(((bf16[8,96,2048]{2,1,0:T(8,128)(2,1)}), bf16[8,96,2048]{2,1,0:T(8,128)(2,1)S(1)}, u32[]{:S(2)}, u32[]{:S(2)}) %all-to-all-start.2) | async-done | bytes 3145760 | tf_op jit(solution)/shard_map/all_to_all | solution.py:570
  264.9 4.5 %all-to-all-start.3 = ((bf16[8,32,2176]{2,1,0:T(8,128)(2,1)}), bf16[8,32,2176]{2,1,0:T(8,128)(2,1)S(1)}, u32[]{:S(2)}, u32[]{:S(2)}) async-start(bf16[8,32,2176]{2,1,0:T(8,128)(2,1)} %shard_map.205), calls=%async_computation.3 | async-start | bytes 2228224 | tf_op jit(solution)/shard_map/all_to_all | solution.py:570
  271.9 18.3 %collective-permute-done.41.refs_1_ = bf16[96,2048]{1,0:T(8,128)(2,1)S(1)} collective-permute-done((bf16[96,2048]{1,0:T(8,128)(2,1)S(1)}, bf16[96,2048]{1,0:T(8,128)(2,1)S(1)}, u32[]{:S(2)}, u32[]{:S(2)}) %collective-permute-start.41) | collective-permute-done | bytes 393248 | tf_op jit(solution)/shard_map/ppermute | solution.py:536
  300.5 17.4 %collective-permute-done.42.refs_1_ = bf16[32,2176]{1,0:T(8,128)(2,1)S(1)} collective-permute-done((bf16[32,2176]{1,0:T(8,128)(2,1)S(1)}, bf16[32,2176]{1,0:T(8,128)(2,1)S(1)}, u32[]{:S(2)}, u32[]{:S(2)}) %collective-permute-start.42) | collective-permute-done | bytes 139296 | tf_op jit(solution)/shard_map/ppermute | solution.py:536
  334.6 4.4 %shard_map.213 = (f32[512,2048]{1,0:T(8,128)}, f32[2048,512]{1,0:T(8,128)}) custom-call(s32[2]{0:T(128)S(1)} %copy-done.44, bf16[512,2048]{1,0:T(8,128)(2,1)S(1)} %copy-done.13, bf16[512,2048]{1,0:T(8,128)(2,1)S(1)} %collective-permute-done.50.other_ref), custom_call_target="tpu_custom_call" | custom-call | flops 4000000000 | tf_op jit(solution)/shard_map/pallas_call | solution.py:517
  (314 shorter events, 127.9 us)
Async XLA Ops:
  17.0 21.8 %collective-permute-start.10 = (bf16[128,2048]{1,0:T(8,128)(2,1)S(1)}, bf16[128,2048]{1,0:T(8,128)(2,1)}, u32[]{:S(2)}, u32[]{:S(2)}) collective-permute-start(bf16[128,2048]{1,0:T(8,128)(2,1)S(1)} %copy-done.15), channel_id=1, source_target_pairs={{0,2},{1,3},{2,0},{3,1},{4,6},{5,7},{6,4},{7,5},{8,10},{9,11},{10,... | collective-permute-start | bytes 1572872 | tf_op jit(solution)/shard_map/ppermute | solution.py:536
  19.1 23.8 %collective-permute-start.13 = (bf16[512,512]{1,0:T(8,128)(2,1)}, bf16[512,512]{1,0:T(8,128)(2,1)}, u32[]{:S(2)}, u32[]{:S(2)}) collective-permute-start(bf16[512,512]{1,0:T(8,128)(2,1)} %refs_4_.3), channel_id=1, source_target_pairs={{0,2},{1,3},{2,0},{3,1},{4,6},{5,7},{6,4},{7,5},{8,10},{9,11},{10,... | collective-permute-start | bytes 1572872 | tf_op jit(solution)/shard_map/ppermute | solution.py:536
  31.5 53.1 %all-to-all-start = ((bf16[8,208,512]{2,1,0:T(8,128)(2,1)}), bf16[8,208,512]{2,1,0:T(8,128)(2,1)S(1)}, u32[]{:S(2)}, u32[]{:S(2)}) async-start(bf16[8,208,512]{2,1,0:T(8,128)(2,1)} %bitcast.12), calls=%async_computation | async-start | bytes 3407872 | tf_op jit(solution)/shard_map/all_to_all | solution.py:674
  75.1 22.2 %collective-permute-start.22 = (bf16[208,512]{1,0:T(8,128)(2,1)}, bf16[208,512]{1,0:T(8,128)(2,1)S(1)}, u32[]{:S(2)}, u32[]{:S(2)}) collective-permute-start(bf16[208,512]{1,0:T(8,128)(2,1)} %get-tuple-element.140), channel_id=1, source_target_pairs={{0,8},{4,12},{8,0},{12,4},{16,24},{20,28},{24,16},{28,20},{1,9},{5... | collective-permute-start | bytes 638984 | tf_op jit(solution)/shard_map/ppermute | solution.py:536
  76.7 21.8 %collective-permute-start.23 = (bf16[208,512]{1,0:T(8,128)(2,1)}, bf16[208,512]{1,0:T(8,128)(2,1)S(1)}, u32[]{:S(2)}, u32[]{:S(2)}) collective-permute-start(bf16[208,512]{1,0:T(8,128)(2,1)} %get-tuple-element.141), channel_id=1, source_target_pairs={{0,12},{4,8},{8,4},{12,0},{16,28},{20,24},{24,20},{28,16},{1,13},{... | collective-permute-start | bytes 638984 | tf_op jit(solution)/shard_map/ppermute | solution.py:536
  76.9 30.9 %collective-permute-start.24 = (bf16[208,512]{1,0:T(8,128)(2,1)}, bf16[208,512]{1,0:T(8,128)(2,1)}, u32[]{:S(2)}, u32[]{:S(2)}) collective-permute-start(bf16[208,512]{1,0:T(8,128)(2,1)} %get-tuple-element.144), channel_id=1, source_target_pairs={{0,16},{4,20},{8,24},{12,28},{16,0},{20,4},{24,8},{28,12},{1,17},{... | collective-permute-start | bytes 638984 | tf_op jit(solution)/shard_map/ppermute | solution.py:536
  79.7 31.1 %collective-permute-start.26 = (bf16[208,512]{1,0:T(8,128)(2,1)}, bf16[208,512]{1,0:T(8,128)(2,1)}, u32[]{:S(2)}, u32[]{:S(2)}) collective-permute-start(bf16[208,512]{1,0:T(8,128)(2,1)} %get-tuple-element.148), channel_id=1, source_target_pairs={{0,20},{4,16},{8,28},{12,24},{16,4},{20,0},{24,12},{28,8},{1,21},{... | collective-permute-start | bytes 638984 | tf_op jit(solution)/shard_map/ppermute | solution.py:536
  81.0 39.6 %collective-permute-start.27 = (bf16[208,512]{1,0:T(8,128)(2,1)}, bf16[208,512]{1,0:T(8,128)(2,1)}, u32[]{:S(2)}, u32[]{:S(2)}) collective-permute-start(bf16[208,512]{1,0:T(8,128)(2,1)} %get-tuple-element.151), channel_id=1, source_target_pairs={{0,24},{4,28},{8,16},{12,20},{16,8},{20,12},{24,0},{28,4},{1,25},{... | collective-permute-start | bytes 638984 | tf_op jit(solution)/shard_map/ppermute | solution.py:536
  97.3 29.8 %collective-permute-start.30 = (bf16[208,512]{1,0:T(8,128)(2,1)S(1)}, bf16[208,512]{1,0:T(8,128)(2,1)S(1)}, u32[]{:S(2)}, u32[]{:S(2)}) collective-permute-start(bf16[208,512]{1,0:T(8,128)(2,1)S(1)} %copy-done.89), channel_id=1, source_target_pairs={{0,28},{4,24},{8,20},{12,16},{16,12},{20,8},{24,4},{28,0},{1,29},{... | collective-permute-start | bytes 638984 | tf_op jit(solution)/shard_map/ppermute | solution.py:536
  120.6 37.8 %collective-permute-start.31 = (bf16[208,512]{1,0:T(8,128)(2,1)}, bf16[208,512]{1,0:T(8,128)(2,1)S(1)}, u32[]{:S(2)}, u32[]{:S(2)}) collective-permute-start(bf16[208,512]{1,0:T(8,128)(2,1)} %get-tuple-element.182), channel_id=1, source_target_pairs={{0,16},{4,20},{8,24},{12,28},{16,0},{20,4},{24,8},{28,12},{1,17},{... | collective-permute-start | bytes 638984 | tf_op jit(solution)/shard_map/ppermute | solution.py:536
  125.8 32.7 %collective-permute-start.32 = (bf16[208,512]{1,0:T(8,128)(2,1)}, bf16[208,512]{1,0:T(8,128)(2,1)S(1)}, u32[]{:S(2)}, u32[]{:S(2)}) collective-permute-start(bf16[208,512]{1,0:T(8,128)(2,1)} %get-tuple-element.183), channel_id=1, source_target_pairs={{0,20},{4,16},{8,28},{12,24},{16,4},{20,0},{24,12},{28,8},{1,21},{... | collective-permute-start | bytes 638984 | tf_op jit(solution)/shard_map/ppermute | solution.py:536
  137.4 21.1 %collective-permute-start.33 = (bf16[208,512]{1,0:T(8,128)(2,1)}, bf16[208,512]{1,0:T(8,128)(2,1)S(1)}, u32[]{:S(2)}, u32[]{:S(2)}) collective-permute-start(bf16[208,512]{1,0:T(8,128)(2,1)} %get-tuple-element.184), channel_id=1, source_target_pairs={{0,24},{4,28},{8,16},{12,20},{16,8},{20,12},{24,0},{28,4},{1,25},{... | collective-permute-start | bytes 638984 | tf_op jit(solution)/shard_map/ppermute | solution.py:536
  137.8 20.7 %collective-permute-start.34 = (bf16[208,512]{1,0:T(8,128)(2,1)}, bf16[208,512]{1,0:T(8,128)(2,1)S(1)}, u32[]{:S(2)}, u32[]{:S(2)}) collective-permute-start(bf16[208,512]{1,0:T(8,128)(2,1)} %get-tuple-element.185), channel_id=1, source_target_pairs={{0,28},{4,24},{8,20},{12,16},{16,12},{20,8},{24,4},{28,0},{1,29},{... | collective-permute-start | bytes 638984 | tf_op jit(solution)/shard_map/ppermute | solution.py:536
  163.6 52.2 %all-to-all-start.1 = ((bf16[8,208,512]{2,1,0:T(8,128)(2,1)}), bf16[8,208,512]{2,1,0:T(8,128)(2,1)S(1)}, u32[]{:S(2)}, u32[]{:S(2)}) async-start(bf16[8,208,512]{2,1,0:T(8,128)(2,1)} %shard_map.196), calls=%async_computation.1 | async-start | bytes 3407872 | tf_op jit(solution)/shard_map/all_to_all | solution.py:771
  176.3 27.6 %collective-permute-start.36 = (bf16[128,2048]{1,0:T(8,128)(2,1)}, bf16[128,2048]{1,0:T(8,128)(2,1)S(1)}, u32[]{:S(2)}, u32[]{:S(2)}) collective-permute-start(bf16[128,2048]{1,0:T(8,128)(2,1)} %get-tuple-element.197.refs_0_), channel_id=1, source_target_pairs={{0,2},{1,3},{2,0},{3,1},{4,6},{5,7},{6,4},{7,5},{8,10},{9,11},{10,... | collective-permute-start | bytes 1572872 | tf_op jit(solution)/shard_map/ppermute | solution.py:536
  177.8 26.8 %collective-permute-start.37 = (bf16[128,2048]{1,0:T(8,128)(2,1)}, bf16[128,2048]{1,0:T(8,128)(2,1)S(1)}, u32[]{:S(2)}, u32[]{:S(2)}) collective-permute-start(bf16[128,2048]{1,0:T(8,128)(2,1)} %get-tuple-element.198.refs_1_), channel_id=1, source_target_pairs={{0,2},{1,3},{2,0},{3,1},{4,6},{5,7},{6,4},{7,5},{8,10},{9,11},{10,... | collective-permute-start | bytes 1572872 | tf_op jit(solution)/shard_map/ppermute | solution.py:536
  217.0 46.8 %all-to-all-start.2 = ((bf16[8,96,2048]{2,1,0:T(8,128)(2,1)}), bf16[8,96,2048]{2,1,0:T(8,128)(2,1)S(1)}, u32[]{:S(2)}, u32[]{:S(2)}) async-start(bf16[8,96,2048]{2,1,0:T(8,128)(2,1)} %shard_map.203), calls=%async_computation.2 | async-start | bytes 6291456 | tf_op jit(solution)/shard_map/all_to_all | solution.py:570
  264.9 28.1 %all-to-all-start.3 = ((bf16[8,32,2176]{2,1,0:T(8,128)(2,1)}), bf16[8,32,2176]{2,1,0:T(8,128)(2,1)S(1)}, u32[]{:S(2)}, u32[]{:S(2)}) async-start(bf16[8,32,2176]{2,1,0:T(8,128)(2,1)} %shard_map.205), calls=%async_computation.3 | async-start | bytes 2228224 | tf_op jit(solution)/shard_map/all_to_all | solution.py:570
  269.5 20.8 %collective-permute-start.41 = (bf16[96,2048]{1,0:T(8,128)(2,1)S(1)}, bf16[96,2048]{1,0:T(8,128)(2,1)S(1)}, u32[]{:S(2)}, u32[]{:S(2)}) collective-permute-start(bf16[96,2048]{1,0:T(8,128)(2,1)S(1)} %copy-done.33), channel_id=1, source_target_pairs={{0,16},{4,20},{8,24},{12,28},{16,0},{20,4},{24,8},{28,12},{1,17},{... | collective-permute-start | bytes 1179656 | tf_op jit(solution)/shard_map/ppermute | solution.py:536
  293.8 25.2 %collective-permute-start.49 = (bf16[256,2048]{1,0:T(8,128)(2,1)S(1)}, bf16[256,2048]{1,0:T(8,128)(2,1)S(1)}, u32[]{:S(2)}, u32[]{:S(2)}) collective-permute-start(bf16[256,2048]{1,0:T(8,128)(2,1)S(1)} %copy-done.14), channel_id=1, source_target_pairs={{0,2},{1,3},{2,0},{3,1},{4,6},{5,7},{6,4},{7,5},{8,10},{9,11},{10,... | collective-permute-start | bytes 3145736 | tf_op jit(solution)/shard_map/ppermute | solution.py:536
  295.5 23.1 %collective-permute-start.46 = (bf16[96,2048]{1,0:T(8,128)(2,1)}, bf16[96,2048]{1,0:T(8,128)(2,1)S(1)}, u32[]{:S(2)}, u32[]{:S(2)}) collective-permute-start(bf16[96,2048]{1,0:T(8,128)(2,1)} %shard_map.209.refs_4_.refs_0_), channel_id=1, source_target_pairs={{0,4},{4,0},{8,12},{12,8},{16,20},{20,16},{24,28},{28,24},{1,5},{5... | collective-permute-start | bytes 1179656 | tf_op jit(solution)/shard_map/ppermute | solution.py:536
  297.0 21.6 %collective-permute-start.47 = (bf16[96,2048]{1,0:T(8,128)(2,1)}, bf16[96,2048]{1,0:T(8,128)(2,1)S(1)}, u32[]{:S(2)}, u32[]{:S(2)}) collective-permute-start(bf16[96,2048]{1,0:T(8,128)(2,1)} %shard_map.209.refs_4_.refs_0_), channel_id=1, source_target_pairs={{0,8},{4,12},{8,0},{12,4},{16,24},{20,28},{24,16},{28,20},{1,9},{5... | collective-permute-start | bytes 1179656 | tf_op jit(solution)/shard_map/ppermute | solution.py:536
  299.4 19.7 %collective-permute-start.48 = (bf16[96,2048]{1,0:T(8,128)(2,1)}, bf16[96,2048]{1,0:T(8,128)(2,1)S(1)}, u32[]{:S(2)}, u32[]{:S(2)}) collective-permute-start(bf16[96,2048]{1,0:T(8,128)(2,1)} %shard_map.209.refs_4_.refs_0_), channel_id=1, source_target_pairs={{0,12},{4,8},{8,4},{12,0},{16,28},{20,24},{24,20},{28,16},{1,13},{... | collective-permute-start | bytes 1179656 | tf_op jit(solution)/shard_map/ppermute | solution.py:536
  299.4 18.5 %collective-permute-start.42 = (bf16[32,2176]{1,0:T(8,128)(2,1)S(1)}, bf16[32,2176]{1,0:T(8,128)(2,1)S(1)}, u32[]{:S(2)}, u32[]{:S(2)}) collective-permute-start(bf16[32,2176]{1,0:T(8,128)(2,1)S(1)} %copy-done.35), channel_id=1, source_target_pairs={{0,16},{4,20},{8,24},{12,28},{16,0},{20,4},{24,8},{28,12},{1,17},{... | collective-permute-start | bytes 417800 | tf_op jit(solution)/shard_map/ppermute | solution.py:536
  (121 other events, 1284.3 us)
where the time goes:
time: 345 us; the launch traced here: 339 us
  Pallas kernels  139 us (40%)
  waiting for transfers between devices  88.3 us (26%)
  starting transfers between devices  74.8 us (22%)
  local copies, waits for them, and re-layouts  34 us (10%)
    pallas_call x23, Pallas kernels, call(): pl.pallas_call(kernel, out_shape=[(pltpu.HBM if rest else jax.ShapeDtypeS...  89 us
    ppermute x51, waiting for transfers between devices, flip(): lax.ppermute(array, axis, [(i, i ^ bit) for i in range(lax.axis_size(axis...  69.6 us
    ppermute x51, starting transfers between devices, flip(): lax.ppermute(array, axis, [(i, i ^ bit) for i in range(lax.axis_size(axis...  50.5 us
    pallas_call x4, Pallas kernels, local(): pl.pallas_call(functools.partial(experts_kernel, slots, per, each), out_s...  37.4 us
    unnamed x180, local copies, waits for them, and re-layouts  23.2 us
    all_to_all x2, waiting for transfers between devices, trade_cube(): lax.all_to_all(blocks, ('expert', 'wshard'), 0, 0, axis_index_groups=grou...  18.6 us
    pallas_call x1, Pallas kernels, local(): pl.pallas_call(functools.partial(expert_grads_kernel, n), grid=(FF // CHU...  13 us
    all_to_all x2, starting transfers between devices, trade_cube(): lax.all_to_all(blocks, ('expert', 'wshard'), 0, 0, axis_index_groups=grou...  9.66 us
  transfers between devices with their start and end apart: 55, of which 19 were waited for; matrix products, arithmetic and copies ran while one was open for 3% of the time, Pallas kernels for 38%

commit v1 on v0

--- a/solution.py
+++ b/solution.py
@@ -201,9 +201,9 @@
     normed = (unit * gain_ref[...]).astype(BF16)
     wait_all(w1_copies)
     total = x_ref[...]
-    for j in range(FF // CHUNK):
-        at = slice(j * CHUNK, (j + 1) * CHUNK)
-        active = gelu(dot(normed, w1_held[:, :, at].reshape(D, CHUNK))).astype(BF16)
+    for j in range(FF // 1024):
+        at = slice(j * 1024, (j + 1) * 1024)
+        active = gelu(dot(normed, w1_held[:, :, at].reshape(D, 1024))).astype(BF16)
         if j == 0:
             wait_all(w2_copies)
         total = total + dot(active, w2_held[...].reshape(FF, D)[at])
@@ -222,9 +222,9 @@
     wait_all(w1_copies)
     wait_all(w2_copies)
     dn = None
-    for j in range(FF // CHUNK):
-        at = slice(j * CHUNK, (j + 1) * CHUNK)
-        w1_now = w1_held[:, :, at].reshape(D, CHUNK)
+    for j in range(FF // 1024):
+        at = slice(j * 1024, (j + 1) * 1024)
+        w1_now = w1_held[:, :, at].reshape(D, 1024)
         w2_now = w2_held[...].reshape(FF, D)[at]
         active, slope = gelu_parts(dot(normed, w1_now))
         dh = (slope * dot(dout, w2_now, 1, 1)).astype(BF16)
@@ -375,8 +375,9 @@
             total1 = part1 if total1 is None else total1 + part1
             total2 = part2 if total2 is None else total2 + part2
         target[0:256] = total1.astype(BF16)
-        target[256:512, 0:256] = total2[0:256].astype(BF16)
-        target[256:512, 256:512] = total2[256:512].astype(BF16)
+        for block in range(total2.shape[0] // 256):
+            rows = slice(block * 256, (block + 1) * 256)
+            target[256:512, rows] = total2[rows].astype(BF16)
 
 
 def cut_kernel(a_ref, b_ref, *outs):
@@ -394,13 +395,19 @@
         row += a_ref.shape[0]
 
 
-def join_kernel(pos_ref, own_ref, other_ref, out1_ref, out2_ref):
+def join_rows_kernel(pos_ref, own_ref, other_ref, out_ref):
+    core = pos_ref[0] & 1
+    for mine, ref in ((core, own_ref), (1 - core, other_ref)):
+        out_ref[pl.ds(pl.multiple_of(mine * 256, 256), 256)] = ref[...].astype(F32)
+
+
+def join_columns_kernel(pos_ref, own_ref, other_ref, out_ref):
     core = pos_ref[0] & 1
     for mine, ref in ((core, own_ref), (1 - core, other_ref)):
         at = pl.ds(pl.multiple_of(mine * 256, 256), 256)
-        out1_ref[at] = ref[0:256].astype(F32)
         for block in range(FF // 256):
-            out2_ref[block * 256 : (block + 1) * 256, at] = ref[256:512, block * 256 : (block + 1) * 256].astype(F32)
+            rows = slice(block * 256, (block + 1) * 256)
+            out_ref[rows, at] = ref[:, rows].astype(F32)
 
 
 def arrange_kernel(pos_ref, *refs):
@@ -710,7 +717,7 @@
         tall = len(count) * slots
         fixed = lambda *shape: pl.BlockSpec(shape, lambda j, pos_ref: (0,) * len(shape))
         source = lambda k: pl.BlockSpec((1, slots, D), lambda j, pos_ref: (pos_ref[1] ^ k, 0, 0))
-        across = lambda height: pl.BlockSpec((height, CHUNK), lambda j, pos_ref: (0, j))
+        across = lambda height: pl.BlockSpec((height, 1024), lambda j, pos_ref: (0, j))
         *made, f, dh, dy = pl.pallas_call(
             functools.partial(experts_kernel, slots, per, each),
             out_shape=[pltpu.HBM((each * slots, D), BF16)] * (2 * per)
@@ -718,8 +725,8 @@
             + [pltpu.HBM((tall, D), BF16)],
             grid_spec=pltpu.PrefetchScalarGridSpec(
                 num_scalar_prefetch=1,
-                grid=(FF // CHUNK,),
-                in_specs=[across(D), pl.BlockSpec((CHUNK, D), lambda j, pos_ref: (j, 0))]
+                grid=(FF // 1024,),
+                in_specs=[across(D), pl.BlockSpec((1024, D), lambda j, pos_ref: (j, 0))]
                 + [source(k) for k in count]
                 + [fixed(each * slots, D)] * per,
                 out_specs=[fixed(each * slots, D)] * (2 * per) + [across(tall)] * 2 + [fixed(tall, D)],
@@ -743,18 +750,18 @@
         z_block = jnp.concatenate(z_out).reshape(experts, slots, D)
     n = len(work)
     whole_rows = lambda a: pl.BlockSpec(a.shape, lambda j: (0, 0))
-    chunk = lambda a: pl.BlockSpec((a.shape[0], CHUNK), lambda j: (0, j))
+    chunk = lambda a: pl.BlockSpec((a.shape[0], 1024), lambda j: (0, j))
     fs, dhs, dys = ([w[i] for w in work] for i in range(3))
     if linked:
         dys[0], *dc_in[per : 2 * per] = lax.optimization_barrier((dys[0], *dc_in[per : 2 * per]))
     grad_send, grad_keep = pl.pallas_call(
         functools.partial(expert_grads_kernel, n),
-        grid=(FF // CHUNK,),
+        grid=(FF // 1024,),
         in_specs=[SCALAR]
         + [whole_rows(a) for a in c_in]
         + [chunk(a) for a in fs + dhs]
         + [whole_rows(a) for a in dys],
-        out_specs=[pl.BlockSpec((512, CHUNK), lambda j: (0, j))] * 2,
+        out_specs=[pl.BlockSpec((512, 1024), lambda j: (0, j))] * 2,
         out_shape=[pltpu.HBM((512, FF), BF16)] * 2,
         cost_estimate=spent(10.0),
         compiler_params=pltpu.CompilerParams(vmem_limit_bytes=VMEM_LIMIT),
@@ -798,16 +805,24 @@
     (final,) = call(final_kernel, [((rows, D), BF16)], z_in.reshape(every, D), x3, turned, us=3.5)
 
     wide = first[0].shape[-1]
+
+    def join(kernel, shape, pieces, came):
+        (half,) = call(glue_kernel, [((256, FF), BF16, AWAY)], *pieces, *came)
+        return call(
+            kernel, [(shape, F32)], pos, half, flip(half, "wshard", 1), specs=[SCALAR] + [WHOLE] * 2, us=2.0
+        )[0]
+
+    expert1 = join(join_rows_kernel, (D, FF), [after(grads[0], dx), grads[1]], crossed)
     if linked:
         tail = split_cube(pos, [(first[0], after(first[1], final))])
         final_rows, input_grad = contract(final, pictures), contract(dx, pictures)
         bulk = sum_cube(after(bulk, tail, final_rows, input_grad))
         deep = flip(bulk, "expert", 4)
-        tail = sum_cube(after(trade_cube(after(tail, bulk)), deep))
+        tail = sum_cube(after(trade_cube(after(tail, bulk)), deep, expert1))
         last = flip(after(grads[2], tail), "wshard", 2)
         bulk = spread(sum_two(bulk, deep))
         tail = sum_two(tail, flip(tail, "expert", 4))
-        crossed.append(after(last, tail, *bulk))
+        last = after(last, tail, *bulk)
         tail = spread(tail)
         mlp1, mlp2 = call(
             finish_mlp_kernel,
@@ -821,6 +836,7 @@
         )
         mlp2 = mlp2.reshape(FF // 4, D)
     else:
+        last = flip(grads[2], "wshard", 2)
         first, second, mlp = sum_plainly(*first), sum_plainly(*second), sum_plainly(*mlp)
         grad_in = jnp.stack([first[:, : 3 * D], second[:, : 3 * D]])
         grad_out = jnp.stack([first[:, 3 * D : 4 * D], second[:, 3 * D :]])
@@ -829,17 +845,7 @@
         final_rows, input_grad = contract(final, pictures), contract(dx, pictures)
         mlp2 = jnp.stack([mlp[64:128], mlp[192:256]]).reshape(2, 64, 4, D).transpose(2, 0, 1, 3).reshape(FF // 4, D)
 
-    if not linked:
-        crossed.append(flip(grads[2], "wshard", 2))
-    (joined,) = call(glue_kernel, [((512, FF), BF16, AWAY)], *grads, *crossed, us=2.0)
-    expert1, expert2 = call(
-        join_kernel,
-        [((D, FF), F32), ((FF, D), F32)],
-        pos, joined, flip(joined, "wshard", 1),
-        specs=[SCALAR] + [WHOLE] * 2,
-        us=4.0,
-    )
-
+    expert2 = join(join_columns_kernel, (FF, D), grads[2:], [last])
     return (
         final_rows,
         input_grad,

time: 345 us -> 341 us (0.988)
  waiting for transfers between devices: 88.3 us -> 84.8 us
    pallas_call x4, Pallas kernels: 37.4 us -> 33.2 us  [local(): pl.pallas_call(functools.partial(experts_kernel, slots, per, each), out_s...]
    ppermute x51 -> x52, waiting for transfers between devices: 69.6 us -> 66.1 us  [flip(): lax.ppermute(array, axis, [(i, i ^ bit) for i in range(lax.axis_size(axis...]
    unnamed x180 -> x184, local copies, waits for them, and re-layouts: 23.2 us -> 24.5 us
    pallas_call x23 -> x25, Pallas kernels: 89 us -> 89.8 us  [call(): pl.pallas_call(kernel, out_shape=[(pltpu.HBM if rest else jax.ShapeDtypeS...]
    ppermute x51 -> x52, starting transfers between devices: 50.5 us -> 51.2 us  [flip(): lax.ppermute(array, axis, [(i, i ^ bit) for i in range(lax.axis_size(axis...]
  transfers between devices with their start and end apart: 55 -> 56, of which waited for: 19 -> 21; matrix products, arithmetic and copies ran while one was open for 3% -> 3% of each run, Pallas kernels for 38% -> 38%
where the time goes in v1:
time: 341 us; the launch traced here: 335 us
  Pallas kernels  136 us (40%)
  waiting for transfers between devices  84.8 us (25%)
  starting transfers between devices  76.4 us (22%)
  local copies, waits for them, and re-layouts  35.2 us (10%)
    pallas_call x25, Pallas kernels, call(): pl.pallas_call(kernel, out_shape=[(pltpu.HBM if rest else jax.ShapeDtypeS...  89.8 us
    ppermute x52, waiting for transfers between devices, flip(): lax.ppermute(array, axis, [(i, i ^ bit) for i in range(lax.axis_size(axis...  66.1 us
    ppermute x52, starting transfers between devices, flip(): lax.ppermute(array, axis, [(i, i ^ bit) for i in range(lax.axis_size(axis...  51.2 us
    pallas_call x4, Pallas kernels, local(): pl.pallas_call(functools.partial(experts_kernel, slots, per, each), out_s...  33.2 us
    unnamed x184, local copies, waits for them, and re-layouts  24.5 us
    all_to_all x2, waiting for transfers between devices, trade_cube(): lax.all_to_all(blocks, ('expert', 'wshard'), 0, 0, axis_index_groups=grou...  18.7 us
    pallas_call x1, Pallas kernels, local(): pl.pallas_call(functools.partial(expert_grads_kernel, n), grid=(FF // 102...  12.6 us
    all_to_all x2, starting transfers between devices, trade_cube(): lax.all_to_all(blocks, ('expert', 'wshard'), 0, 0, axis_index_groups=grou...  9.76 us
  transfers between devices with their start and end apart: 56, of which 21 were waited for; matrix products, arithmetic and copies ran while one was open for 3% of the time, Pallas kernels for 38%

profile of v1, /device:TPU:0, one launch (start us, length us, event | category | flops | bytes accessed | tf_op | source)
XLA Modules:
  0.0 334.8 jit_solution(5293692921866802372)
XLA Ops:
  8.0 7.0 %collective-permute-done.1.refs_2_ = bf16[16,128]{1,0:T(8,128)(2,1)S(1)} collective-permute-done((bf16[16,128]{1,0:T(8,128)(2,1)S(1)}, bf16[16,128]{1,0:T(8,128)(2,1)S(1)}, u32[]{:S(2)}, u32[]{:S(2)}) %collective-permute-start.1) | collective-permute-done | bytes 4128 | tf_op jit(solution)/shard_map/ppermute | solution.py:543
  19.3 5.6 %shard_map.187 = (f32[416,512]{1,0:T(8,128)S(1)}, bf16[416,1536]{1,0:T(8,128)(2,1)S(1)}, bf16[416,512]{1,0:T(8,128)(2,1)S(1)}) custom-call(s32[2]{0:T(128)S(1)} %pad_add_fusion.pos_ref, bf16[416,512]{1,0:T(8,128)(2,1)S(1)} %bitcast.27, f32[1,512]{1,0:T(1,128)S(1)} %get-tuple-element.239.gain_ref, bf16[128,1536]{1,0:T(8,128)(2,1)S(1)} %get-tuple-element.233.refs_0_, ...), custom_call_target="tpu_custom_call" | custom-call | flops 7000000000 | tf_op jit(solution)/shard_map/pallas_call | solution.py:524
  31.5 6.4 %all-to-all-start = ((bf16[8,208,512]{2,1,0:T(8,128)(2,1)}), bf16[8,208,512]{2,1,0:T(8,128)(2,1)S(1)}, u32[]{:S(2)}, u32[]{:S(2)}) async-start(bf16[8,208,512]{2,1,0:T(8,128)(2,1)} %bitcast.12), calls=%async_computation | async-start | bytes 3407872 | tf_op jit(solution)/shard_map/all_to_all | solution.py:681
  38.6 4.3 %collective-permute-done.13.refs_6_ = bf16[512,512]{1,0:T(8,128)(2,1)} collective-permute-done((bf16[512,512]{1,0:T(8,128)(2,1)}, bf16[512,512]{1,0:T(8,128)(2,1)}, u32[]{:S(2)}, u32[]{:S(2)}) %collective-permute-start.13) | collective-permute-done | bytes 524320 | tf_op jit(solution)/shard_map/ppermute | solution.py:543
  46.9 4.4 %shard_map.188.x_ref = f32[416,512]{1,0:T(8,128)S(1)} custom-call(s32[2]{0:T(128)S(1)} %pad_add_fusion.pos_ref, f32[416,512]{1,0:T(8,128)S(1)} %copy-done.70, f32[1,512]{1,0:T(1,128)S(1)} %get-tuple-element.238.gain_ref, bf16[128,2048]{1,0:T(8,128)(2,1)S(1)} %copy-done.16, bf16[128,2048]{1,0:T(8,128)(2,1)S(1)} %collective-permute-done.9.refs_1_, ...), custom_call_target="tpu_custom_call" | custom-call | flops 6499999744 | tf_op jit(solution)/shard_map/pallas_call | solution.py:524
  56.5 3.9 %collective-permute-done.19.refs_6_ = bf16[128,512]{1,0:T(8,128)(2,1)S(1)} collective-permute-done((bf16[128,512]{1,0:T(8,128)(2,1)S(1)}, bf16[128,512]{1,0:T(8,128)(2,1)S(1)}, u32[]{:S(2)}, u32[]{:S(2)}) %collective-permute-start.19) | collective-permute-done | bytes 131104 | tf_op jit(solution)/shard_map/ppermute | solution.py:543
  61.8 5.6 %shard_map.189 = (f32[416,512]{1,0:T(8,128)S(1)}, bf16[416,1536]{1,0:T(8,128)(2,1)S(1)}, bf16[416,512]{1,0:T(8,128)(2,1)S(1)}) custom-call(s32[2]{0:T(128)S(1)} %pad_add_fusion.pos_ref, f32[416,512]{1,0:T(8,128)S(1)} %shard_map.188.x_ref, f32[1,512]{1,0:T(1,128)S(1)} %get-tuple-element.237.gain_ref, bf16[128,1536]{1,0:T(8,128)(2,1)S(1)} %get-tuple-element.126.refs_0_, ...), custom_call_target="tpu_custom_call" | custom-call | flops 7000000000 | tf_op jit(solution)/shard_map/pallas_call | solution.py:524
  88.7 7.9 %shard_map.192 = (bf16[208,512]{1,0:T(8,128)(2,1)}, bf16[208,512]{1,0:T(8,128)(2,1)}, bf16[208,512]{1,0:T(8,128)(2,1)}, bf16[208,512]{1,0:T(8,128)(2,1)}, bf16[4...) custom-call(s32[2]{0:T(128)S(1)} %pad_add_fusion.pos_ref, ...), custom_call_target="tpu_custom_call" | custom-call | flops 8000000000 | tf_op jit(solution)/shard_map/pallas_call | solution.py:721
  98.4 7.6 %shard_map.193 = (bf16[208,512]{1,0:T(8,128)(2,1)}, bf16[208,512]{1,0:T(8,128)(2,1)}, bf16[208,512]{1,0:T(8,128)(2,1)}, bf16[208,512]{1,0:T(8,128)(2,1)}, bf16[4...) custom-call(s32[2]{0:T(128)S(1)} %pad_add_fusion.pos_ref, ...), custom_call_target="tpu_custom_call" | custom-call | flops 8000000000 | tf_op jit(solution)/shard_map/pallas_call | solution.py:721
  106.1 3.9 %collective-permute-done.25.refs_1_ = bf16[208,512]{1,0:T(8,128)(2,1)S(1)} collective-permute-done((bf16[208,512]{1,0:T(8,128)(2,1)}, bf16[208,512]{1,0:T(8,128)(2,1)S(1)}, u32[]{:S(2)}, u32[]{:S(2)}) %collective-permute-start.25) | collective-permute-done | bytes 213024 | tf_op jit(solution)/shard_map/ppermute | solution.py:543
  110.3 8.7 %shard_map.194 = (bf16[208,512]{1,0:T(8,128)(2,1)}, bf16[208,512]{1,0:T(8,128)(2,1)}, bf16[208,512]{1,0:T(8,128)(2,1)}, bf16[208,512]{1,0:T(8,128)(2,1)}, bf16[4...) custom-call(s32[2]{0:T(128)S(1)} %pad_add_fusion.pos_ref, ...), custom_call_target="tpu_custom_call" | custom-call | flops 8000000000 | tf_op jit(solution)/shard_map/pallas_call | solution.py:721
  119.0 5.0 %collective-permute-start.31 = (bf16[208,512]{1,0:T(8,128)(2,1)}, bf16[208,512]{1,0:T(8,128)(2,1)S(1)}, u32[]{:S(2)}, u32[]{:S(2)}) collective-permute-start(bf16[208,512]{1,0:T(8,128)(2,1)} %get-tuple-element.181), channel_id=1, source_target_pairs={{0,16},{4,20},{8,24},{12,28},{16,0},{20,4},{24,8},{28,12},{1,17},{... | collective-permute-start | bytes 638984 | tf_op jit(solution)/shard_map/ppermute | solution.py:543
  125.7 9.0 %shard_map.195 = (bf16[208,512]{1,0:T(8,128)(2,1)}, bf16[208,512]{1,0:T(8,128)(2,1)}, bf16[208,512]{1,0:T(8,128)(2,1)}, bf16[208,512]{1,0:T(8,128)(2,1)}, bf16[4...) custom-call(s32[2]{0:T(128)S(1)} %pad_add_fusion.pos_ref, ...), custom_call_target="tpu_custom_call" | custom-call | flops 8000000000 | tf_op jit(solution)/shard_map/pallas_call | solution.py:721
  141.0 12.6 %shard_map.197 = (bf16[512,2048]{1,0:T(8,128)(2,1)}, bf16[512,2048]{1,0:T(8,128)(2,1)}) custom-call(s32[2]{0:T(128)S(1)} %pad_add_fusion.pos_ref, bf16[208,512]{1,0:T(8,128)(2,1)S(1)} %copy-done.81, bf16[208,512]{1,0:T(8,128)(2,1)S(1)} %collective-permute-done.21.refs_3_.refs_1_, bf16[208,512]{1,0:T(8,128)(2,1)S(1)} %collective-permute-done.22.refs_2_, ...), custom_call_target="tpu_custom_call" | custom-call | flops 10000000000 | tf_op jit(solution)/shard_map/pallas_call | solution.py:757
  160.7 9.0 %all-to-all-start.1 = ((bf16[8,208,512]{2,1,0:T(8,128)(2,1)}), bf16[8,208,512]{2,1,0:T(8,128)(2,1)S(1)}, u32[]{:S(2)}, u32[]{:S(2)}) async-start(bf16[8,208,512]{2,1,0:T(8,128)(2,1)} %shard_map.196), calls=%async_computation.1 | async-start | bytes 3407872 | tf_op jit(solution)/shard_map/all_to_all | solution.py:778
  176.4 12.5 %shard_map.201 = (f32[416,512]{1,0:T(8,128)}, f32[1,512]{1,0:T(1,128)}, bf16[2,2,64,2048]{3,2,1,0:T(8,128)(2,1)}, bf16[2,2,64,2048]{3,2,1,0:T(8,128)(2,1)}) custom-call(s32[2]{0:T(128)} %copy-done.44, f32[416,512]{1,0:T(8,128)} %copy-done.71, f32[1,512]{1,0:T(1,128)} %copy-done.9, bf16[416,1536]{1,0:T(8,128)(2,1)} %copy-done.72, ...), custom_call_target="tpu_custom_call" | custom-call | flops 12499999744 | tf_op jit(solution)/shard_map/pallas_call | solution.py:524
  188.9 12.1 %shard_map.202 = (f32[416,512]{1,0:T(8,128)}, f32[1,512]{1,0:T(1,128)}, bf16[2,2,128,2048]{3,2,1,0:T(8,128)(2,1)}, bf16[2,2,128,2048]{3,2,1,0:T(8,128)(2,1)}) custom-call(s32[2]{0:T(128)} %copy-done.44, f32[416,512]{1,0:T(8,128)} %copy-done.69, f32[1,512]{1,0:T(1,128)} %copy-done.8, f32[416,512]{1,0:T(8,128)} %get-tuple-element.200.dz_ref, ...), custom_call_target="tpu_custom_call" | custom-call | flops 12499999744 | tf_op jit(solution)/shard_map/pallas_call | solution.py:524
  203.1 4.8 %collective-permute-done.38.refs_2_ = bf16[2,2,64,2048]{3,2,1,0:T(8,128)(2,1)S(1)} collective-permute-done((bf16[2,2,64,2048]{3,2,1,0:T(8,128)(2,1)S(1)}, bf16[2,2,64,2048]{3,2,1,0:T(8,128)(2,1)S(1)}, u32[]{:S(2)}, u32[]{:S(2)}) %collective-permute-start.38) | collective-permute-done | bytes 1048608 | tf_op jit(solution)/shard_map/ppermute | solution.py:543
  214.2 5.2 %all-to-all-start.2 = ((bf16[8,96,2048]{2,1,0:T(8,128)(2,1)}), bf16[8,96,2048]{2,1,0:T(8,128)(2,1)S(1)}, u32[]{:S(2)}, u32[]{:S(2)}) async-start(bf16[8,96,2048]{2,1,0:T(8,128)(2,1)} %shard_map.203), calls=%async_computation.2 | async-start | bytes 6291456 | tf_op jit(solution)/shard_map/all_to_all | solution.py:577
  219.4 12.9 %shard_map.204 = (f32[416,512]{1,0:T(8,128)}, f32[1,512]{1,0:T(1,128)}, bf16[2,2,64,2176]{3,2,1,0:T(8,128)(2,1)}, bf16[2,2,64,2176]{3,2,1,0:T(8,128)(2,1)}) custom-call(s32[2]{0:T(128)} %copy-done.44, bf16[416,512]{1,0:T(8,128)(2,1)} %bitcast.28, f32[1,512]{1,0:T(1,128)} %copy-done.7, bf16[416,1536]{1,0:T(8,128)(2,1)} %copy-done.73, ...), custom_call_target="tpu_custom_call" | custom-call | flops 12499999744 | tf_op jit(solution)/shard_map/pallas_call | solution.py:524
  245.1 15.9 %all-to-all-done.2.a_ref = bf16[8,96,2048]{2,1,0:T(8,128)(2,1)S(1)} async-done(((bf16[8,96,2048]{2,1,0:T(8,128)(2,1)}), bf16[8,96,2048]{2,1,0:T(8,128)(2,1)S(1)}, u32[]{:S(2)}, u32[]{:S(2)}) %all-to-all-start.2) | async-done | bytes 3145760 | tf_op jit(solution)/shard_map/all_to_all | solution.py:577
  262.2 4.6 %all-to-all-start.3 = ((bf16[8,32,2176]{2,1,0:T(8,128)(2,1)}), bf16[8,32,2176]{2,1,0:T(8,128)(2,1)S(1)}, u32[]{:S(2)}, u32[]{:S(2)}) async-start(bf16[8,32,2176]{2,1,0:T(8,128)(2,1)} %shard_map.205), calls=%async_computation.3 | async-start | bytes 2228224 | tf_op jit(solution)/shard_map/all_to_all | solution.py:577
  275.0 12.7 %collective-permute-done.41.refs_1_ = bf16[96,2048]{1,0:T(8,128)(2,1)S(1)} collective-permute-done((bf16[96,2048]{1,0:T(8,128)(2,1)S(1)}, bf16[96,2048]{1,0:T(8,128)(2,1)S(1)}, u32[]{:S(2)}, u32[]{:S(2)}) %collective-permute-start.41) | collective-permute-done | bytes 393248 | tf_op jit(solution)/shard_map/ppermute | solution.py:543
  297.9 17.2 %collective-permute-done.43.refs_1_ = bf16[32,2176]{1,0:T(8,128)(2,1)S(1)} collective-permute-done((bf16[32,2176]{1,0:T(8,128)(2,1)S(1)}, bf16[32,2176]{1,0:T(8,128)(2,1)S(1)}, u32[]{:S(2)}, u32[]{:S(2)}) %collective-permute-start.43) | collective-permute-done | bytes 139296 | tf_op jit(solution)/shard_map/ppermute | solution.py:543
  (322 shorter events, 134.1 us)
Async XLA Ops:
  17.0 21.5 %collective-permute-start.10 = (bf16[128,2048]{1,0:T(8,128)(2,1)S(1)}, bf16[128,2048]{1,0:T(8,128)(2,1)}, u32[]{:S(2)}, u32[]{:S(2)}) collective-permute-start(bf16[128,2048]{1,0:T(8,128)(2,1)S(1)} %copy-done.16), channel_id=1, source_target_pairs={{0,2},{1,3},{2,0},{3,1},{4,6},{5,7},{6,4},{7,5},{8,10},{9,11},{10,... | collective-permute-start | bytes 1572872 | tf_op jit(solution)/shard_map/ppermute | solution.py:543
  19.1 23.8 %collective-permute-start.13 = (bf16[512,512]{1,0:T(8,128)(2,1)}, bf16[512,512]{1,0:T(8,128)(2,1)}, u32[]{:S(2)}, u32[]{:S(2)}) collective-permute-start(bf16[512,512]{1,0:T(8,128)(2,1)} %refs_4_.3), channel_id=1, source_target_pairs={{0,2},{1,3},{2,0},{3,1},{4,6},{5,7},{6,4},{7,5},{8,10},{9,11},{10,... | collective-permute-start | bytes 1572872 | tf_op jit(solution)/shard_map/ppermute | solution.py:543
  31.5 53.1 %all-to-all-start = ((bf16[8,208,512]{2,1,0:T(8,128)(2,1)}), bf16[8,208,512]{2,1,0:T(8,128)(2,1)S(1)}, u32[]{:S(2)}, u32[]{:S(2)}) async-start(bf16[8,208,512]{2,1,0:T(8,128)(2,1)} %bitcast.12), calls=%async_computation | async-start | bytes 3407872 | tf_op jit(solution)/shard_map/all_to_all | solution.py:681
  75.0 21.6 %collective-permute-start.22 = (bf16[208,512]{1,0:T(8,128)(2,1)}, bf16[208,512]{1,0:T(8,128)(2,1)S(1)}, u32[]{:S(2)}, u32[]{:S(2)}) collective-permute-start(bf16[208,512]{1,0:T(8,128)(2,1)} %get-tuple-element.139), channel_id=1, source_target_pairs={{0,8},{4,12},{8,0},{12,4},{16,24},{20,28},{24,16},{28,20},{1,9},{5... | collective-permute-start | bytes 638984 | tf_op jit(solution)/shard_map/ppermute | solution.py:543
  76.7 21.2 %collective-permute-start.23 = (bf16[208,512]{1,0:T(8,128)(2,1)}, bf16[208,512]{1,0:T(8,128)(2,1)S(1)}, u32[]{:S(2)}, u32[]{:S(2)}) collective-permute-start(bf16[208,512]{1,0:T(8,128)(2,1)} %get-tuple-element.140), channel_id=1, source_target_pairs={{0,12},{4,8},{8,4},{12,0},{16,28},{20,24},{24,20},{28,16},{1,13},{... | collective-permute-start | bytes 638984 | tf_op jit(solution)/shard_map/ppermute | solution.py:543
  76.9 29.1 %collective-permute-start.24 = (bf16[208,512]{1,0:T(8,128)(2,1)}, bf16[208,512]{1,0:T(8,128)(2,1)}, u32[]{:S(2)}, u32[]{:S(2)}) collective-permute-start(bf16[208,512]{1,0:T(8,128)(2,1)} %get-tuple-element.143), channel_id=1, source_target_pairs={{0,16},{4,20},{8,24},{12,28},{16,0},{20,4},{24,8},{28,12},{1,17},{... | collective-permute-start | bytes 638984 | tf_op jit(solution)/shard_map/ppermute | solution.py:543
  79.7 30.6 %collective-permute-start.26 = (bf16[208,512]{1,0:T(8,128)(2,1)}, bf16[208,512]{1,0:T(8,128)(2,1)}, u32[]{:S(2)}, u32[]{:S(2)}) collective-permute-start(bf16[208,512]{1,0:T(8,128)(2,1)} %get-tuple-element.147), channel_id=1, source_target_pairs={{0,20},{4,16},{8,28},{12,24},{16,4},{20,0},{24,12},{28,8},{1,21},{... | collective-permute-start | bytes 638984 | tf_op jit(solution)/shard_map/ppermute | solution.py:543
  81.0 38.0 %collective-permute-start.27 = (bf16[208,512]{1,0:T(8,128)(2,1)}, bf16[208,512]{1,0:T(8,128)(2,1)}, u32[]{:S(2)}, u32[]{:S(2)}) collective-permute-start(bf16[208,512]{1,0:T(8,128)(2,1)} %get-tuple-element.150), channel_id=1, source_target_pairs={{0,24},{4,28},{8,16},{12,20},{16,8},{20,12},{24,0},{28,4},{1,25},{... | collective-permute-start | bytes 638984 | tf_op jit(solution)/shard_map/ppermute | solution.py:543
  96.7 29.0 %collective-permute-start.30 = (bf16[208,512]{1,0:T(8,128)(2,1)S(1)}, bf16[208,512]{1,0:T(8,128)(2,1)S(1)}, u32[]{:S(2)}, u32[]{:S(2)}) collective-permute-start(bf16[208,512]{1,0:T(8,128)(2,1)S(1)} %copy-done.91), channel_id=1, source_target_pairs={{0,28},{4,24},{8,20},{12,16},{16,12},{20,8},{24,4},{28,0},{1,29},{... | collective-permute-start | bytes 638984 | tf_op jit(solution)/shard_map/ppermute | solution.py:543
  119.0 36.6 %collective-permute-start.31 = (bf16[208,512]{1,0:T(8,128)(2,1)}, bf16[208,512]{1,0:T(8,128)(2,1)S(1)}, u32[]{:S(2)}, u32[]{:S(2)}) collective-permute-start(bf16[208,512]{1,0:T(8,128)(2,1)} %get-tuple-element.181), channel_id=1, source_target_pairs={{0,16},{4,20},{8,24},{12,28},{16,0},{20,4},{24,8},{28,12},{1,17},{... | collective-permute-start | bytes 638984 | tf_op jit(solution)/shard_map/ppermute | solution.py:543
  124.0 31.6 %collective-permute-start.32 = (bf16[208,512]{1,0:T(8,128)(2,1)}, bf16[208,512]{1,0:T(8,128)(2,1)S(1)}, u32[]{:S(2)}, u32[]{:S(2)}) collective-permute-start(bf16[208,512]{1,0:T(8,128)(2,1)} %get-tuple-element.182), channel_id=1, source_target_pairs={{0,20},{4,16},{8,28},{12,24},{16,4},{20,0},{24,12},{28,8},{1,21},{... | collective-permute-start | bytes 638984 | tf_op jit(solution)/shard_map/ppermute | solution.py:543
  134.7 20.9 %collective-permute-start.33 = (bf16[208,512]{1,0:T(8,128)(2,1)}, bf16[208,512]{1,0:T(8,128)(2,1)S(1)}, u32[]{:S(2)}, u32[]{:S(2)}) collective-permute-start(bf16[208,512]{1,0:T(8,128)(2,1)} %get-tuple-element.183), channel_id=1, source_target_pairs={{0,24},{4,28},{8,16},{12,20},{16,8},{20,12},{24,0},{28,4},{1,25},{... | collective-permute-start | bytes 638984 | tf_op jit(solution)/shard_map/ppermute | solution.py:543
  135.0 20.6 %collective-permute-start.34 = (bf16[208,512]{1,0:T(8,128)(2,1)}, bf16[208,512]{1,0:T(8,128)(2,1)S(1)}, u32[]{:S(2)}, u32[]{:S(2)}) collective-permute-start(bf16[208,512]{1,0:T(8,128)(2,1)} %get-tuple-element.184), channel_id=1, source_target_pairs={{0,28},{4,24},{8,20},{12,16},{16,12},{20,8},{24,4},{28,0},{1,29},{... | collective-permute-start | bytes 638984 | tf_op jit(solution)/shard_map/ppermute | solution.py:543
  160.7 52.4 %all-to-all-start.1 = ((bf16[8,208,512]{2,1,0:T(8,128)(2,1)}), bf16[8,208,512]{2,1,0:T(8,128)(2,1)S(1)}, u32[]{:S(2)}, u32[]{:S(2)}) async-start(bf16[8,208,512]{2,1,0:T(8,128)(2,1)} %shard_map.196), calls=%async_computation.1 | async-start | bytes 3407872 | tf_op jit(solution)/shard_map/all_to_all | solution.py:778
  174.4 26.7 %collective-permute-start.36 = (bf16[128,2048]{1,0:T(8,128)(2,1)}, bf16[128,2048]{1,0:T(8,128)(2,1)S(1)}, u32[]{:S(2)}, u32[]{:S(2)}) collective-permute-start(bf16[128,2048]{1,0:T(8,128)(2,1)} %get-tuple-element.221.refs_0_), channel_id=1, source_target_pairs={{0,2},{1,3},{2,0},{3,1},{4,6},{5,7},{6,4},{7,5},{8,10},{9,11},{10,... | collective-permute-start | bytes 1572872 | tf_op jit(solution)/shard_map/ppermute | solution.py:543
  175.9 26.0 %collective-permute-start.37 = (bf16[128,2048]{1,0:T(8,128)(2,1)}, bf16[128,2048]{1,0:T(8,128)(2,1)S(1)}, u32[]{:S(2)}, u32[]{:S(2)}) collective-permute-start(bf16[128,2048]{1,0:T(8,128)(2,1)} %get-tuple-element.197.refs_1_), channel_id=1, source_target_pairs={{0,2},{1,3},{2,0},{3,1},{4,6},{5,7},{6,4},{7,5},{8,10},{9,11},{10,... | collective-permute-start | bytes 1572872 | tf_op jit(solution)/shard_map/ppermute | solution.py:543
  214.2 46.8 %all-to-all-start.2 = ((bf16[8,96,2048]{2,1,0:T(8,128)(2,1)}), bf16[8,96,2048]{2,1,0:T(8,128)(2,1)S(1)}, u32[]{:S(2)}, u32[]{:S(2)}) async-start(bf16[8,96,2048]{2,1,0:T(8,128)(2,1)} %shard_map.203), calls=%async_computation.2 | async-start | bytes 6291456 | tf_op jit(solution)/shard_map/all_to_all | solution.py:577
  262.2 28.3 %all-to-all-start.3 = ((bf16[8,32,2176]{2,1,0:T(8,128)(2,1)}), bf16[8,32,2176]{2,1,0:T(8,128)(2,1)S(1)}, u32[]{:S(2)}, u32[]{:S(2)}) async-start(bf16[8,32,2176]{2,1,0:T(8,128)(2,1)} %shard_map.205), calls=%async_computation.3 | async-start | bytes 2228224 | tf_op jit(solution)/shard_map/all_to_all | solution.py:577
  268.0 19.6 %collective-permute-start.41 = (bf16[96,2048]{1,0:T(8,128)(2,1)S(1)}, bf16[96,2048]{1,0:T(8,128)(2,1)S(1)}, u32[]{:S(2)}, u32[]{:S(2)}) collective-permute-start(bf16[96,2048]{1,0:T(8,128)(2,1)S(1)} %copy-done.34), channel_id=1, source_target_pairs={{0,16},{4,20},{8,24},{12,28},{16,0},{20,4},{24,8},{28,12},{1,17},{... | collective-permute-start | bytes 1179656 | tf_op jit(solution)/shard_map/ppermute | solution.py:543
  291.3 25.1 %collective-permute-start.50 = (bf16[256,2048]{1,0:T(8,128)(2,1)S(1)}, bf16[256,2048]{1,0:T(8,128)(2,1)S(1)}, u32[]{:S(2)}, u32[]{:S(2)}) collective-permute-start(bf16[256,2048]{1,0:T(8,128)(2,1)S(1)} %copy-done.13), channel_id=1, source_target_pairs={{0,2},{1,3},{2,0},{3,1},{4,6},{5,7},{6,4},{7,5},{8,10},{9,11},{10,... | collective-permute-start | bytes 3145736 | tf_op jit(solution)/shard_map/ppermute | solution.py:543
  292.8 23.1 %collective-permute-start.47 = (bf16[96,2048]{1,0:T(8,128)(2,1)}, bf16[96,2048]{1,0:T(8,128)(2,1)S(1)}, u32[]{:S(2)}, u32[]{:S(2)}) collective-permute-start(bf16[96,2048]{1,0:T(8,128)(2,1)} %shard_map.211.refs_4_.refs_0_), channel_id=1, source_target_pairs={{0,4},{4,0},{8,12},{12,8},{16,20},{20,16},{24,28},{28,24},{1,5},{5... | collective-permute-start | bytes 1179656 | tf_op jit(solution)/shard_map/ppermute | solution.py:543
  294.3 21.6 %collective-permute-start.48 = (bf16[96,2048]{1,0:T(8,128)(2,1)}, bf16[96,2048]{1,0:T(8,128)(2,1)S(1)}, u32[]{:S(2)}, u32[]{:S(2)}) collective-permute-start(bf16[96,2048]{1,0:T(8,128)(2,1)} %shard_map.211.refs_4_.refs_0_), channel_id=1, source_target_pairs={{0,8},{4,12},{8,0},{12,4},{16,24},{20,28},{24,16},{28,20},{1,9},{5... | collective-permute-start | bytes 1179656 | tf_op jit(solution)/shard_map/ppermute | solution.py:543
  296.7 19.7 %collective-permute-start.49 = (bf16[96,2048]{1,0:T(8,128)(2,1)}, bf16[96,2048]{1,0:T(8,128)(2,1)S(1)}, u32[]{:S(2)}, u32[]{:S(2)}) collective-permute-start(bf16[96,2048]{1,0:T(8,128)(2,1)} %shard_map.211.refs_4_.refs_0_), channel_id=1, source_target_pairs={{0,12},{4,8},{8,4},{12,0},{16,28},{20,24},{24,20},{28,16},{1,13},{... | collective-permute-start | bytes 1179656 | tf_op jit(solution)/shard_map/ppermute | solution.py:543
  296.7 18.5 %collective-permute-start.43 = (bf16[32,2176]{1,0:T(8,128)(2,1)S(1)}, bf16[32,2176]{1,0:T(8,128)(2,1)S(1)}, u32[]{:S(2)}, u32[]{:S(2)}) collective-permute-start(bf16[32,2176]{1,0:T(8,128)(2,1)S(1)} %copy-done.37), channel_id=1, source_target_pairs={{0,16},{4,20},{8,24},{12,28},{16,0},{20,4},{24,8},{28,12},{1,17},{... | collective-permute-start | bytes 417800 | tf_op jit(solution)/shard_map/ppermute | solution.py:543
  (124 other events, 1201.3 us)

commit v2 on v1

--- a/solution.py
+++ b/solution.py
@@ -324,7 +324,7 @@
     def _():
         for b, here in blocks:
             end = (b % each + 1) * slots
-            gate = read_spare(c_refs[b // each][end - 8 : end].astype(F32), slots)
+            gate = read_spare(c_refs[b // each][end - 16 : end].astype(F32)[8:], slots)
             gate_ref[here] = jnp.broadcast_to(gate, (slots, 128))
             dy_ref[here] = (gate * g_refs[b][0].astype(F32)).astype(BF16)
 
@@ -439,7 +439,7 @@
         part = dot(jnp.where(hit, 1.0, 0.0).astype(BF16), block)
         gc = part if gc is None else gc + part
         place = lax.broadcasted_iota(jnp.int32, (slots, tokens), 0) + start
-        column = read_spare(block[slots - 8 :].astype(F32), slots)
+        column = read_spare(block[slots - 16 :].astype(F32)[8:], slots)
         for j in range(TOP):
             hit = place == index_ref[j : j + 1, :]
             dgates[j] = dgates[j] + jnp.sum(jnp.where(hit, column, 0.0), axis=0, keepdims=True)
@@ -733,7 +733,7 @@
                 scratch_shapes=[pltpu.VMEM((tall, 128), F32), pltpu.VMEM((tall, D), F32), pltpu.VMEM((tall, D), F32)],
             ),
             cost_estimate=spent(8.0),
-            compiler_params=pltpu.CompilerParams(vmem_limit_bytes=VMEM_LIMIT),
+            compiler_params=pltpu.CompilerParams(vmem_limit_bytes=VMEM_LIMIT if first else 58 * 1024 * 1024),
         )(pos, expert_in[0], expert_out[0], *[g_in] * len(count), *given)
         dc_out += made[:per]
         z_out += made[per:]

time: 341 us -> 339 us (level)
  waiting for transfers between devices: 84.8 us -> 80.7 us
    ppermute x52, waiting for transfers between devices: 66.1 us -> 61.9 us  [flip(): lax.ppermute(array, axis, [(i, i ^ bit) for i in range(lax.axis_size(axis...]
    unnamed x184 -> x190, local copies, waits for them, and re-layouts: 24.5 us -> 26 us
  transfers between devices with their start and end apart: 56 -> 56, of which waited for: 21 -> 19; matrix products, arithmetic and copies ran while one was open for 3% -> 3% of each run, Pallas kernels for 38% -> 39%
where the time goes in v2:
time: 339 us; the launch traced here: 333 us
  Pallas kernels  138 us (41%)
  waiting for transfers between devices  80.7 us (24%)
  starting transfers between devices  75 us (22%)
  local copies, waits for them, and re-layouts  36.8 us (11%)
    pallas_call x25, Pallas kernels, call(): pl.pallas_call(kernel, out_shape=[(pltpu.HBM if rest else jax.ShapeDtypeS...  89.8 us
    ppermute x52, waiting for transfers between devices, flip(): lax.ppermute(array, axis, [(i, i ^ bit) for i in range(lax.axis_size(axis...  61.9 us
    ppermute x52, starting transfers between devices, flip(): lax.ppermute(array, axis, [(i, i ^ bit) for i in range(lax.axis_size(axis...  52.6 us
    pallas_call x4, Pallas kernels, local(): pl.pallas_call(functools.partial(experts_kernel, slots, per, each), out_s...  35.2 us
    unnamed x190, local copies, waits for them, and re-layouts  26 us
    all_to_all x2, waiting for transfers between devices, trade_cube(): lax.all_to_all(blocks, ('expert', 'wshard'), 0, 0, axis_index_groups=grou...  18.7 us
    pallas_call x1, Pallas kernels, local(): pl.pallas_call(functools.partial(expert_grads_kernel, n), grid=(FF // 102...  12.5 us
    all_to_all x2, starting transfers between devices, trade_cube(): lax.all_to_all(blocks, ('expert', 'wshard'), 0, 0, axis_index_groups=grou...  9.76 us
  transfers between devices with their start and end apart: 56, of which 19 were waited for; matrix products, arithmetic and copies ran while one was open for 3% of the time, Pallas kernels for 39%

profile of v2, /device:TPU:0, one launch (start us, length us, event | category | flops | bytes accessed | tf_op | source)
XLA Modules:
  0.0 332.8 jit_solution(16837147687369071719)
XLA Ops:
  8.0 7.0 %collective-permute-done.1.refs_2_ = bf16[16,128]{1,0:T(8,128)(2,1)S(1)} collective-permute-done((bf16[16,128]{1,0:T(8,128)(2,1)S(1)}, bf16[16,128]{1,0:T(8,128)(2,1)S(1)}, u32[]{:S(2)}, u32[]{:S(2)}) %collective-permute-start.1) | collective-permute-done | bytes 4128 | tf_op jit(solution)/shard_map/ppermute | solution.py:543
  19.3 5.6 %shard_map.187 = (f32[416,512]{1,0:T(8,128)S(1)}, bf16[416,1536]{1,0:T(8,128)(2,1)S(1)}, bf16[416,512]{1,0:T(8,128)(2,1)S(1)}) custom-call(s32[2]{0:T(128)S(1)} %pad_add_fusion.pos_ref, bf16[416,512]{1,0:T(8,128)(2,1)S(1)} %bitcast.27, f32[1,512]{1,0:T(1,128)S(1)} %get-tuple-element.239.gain_ref, bf16[128,1536]{1,0:T(8,128)(2,1)S(1)} %get-tuple-element.233.refs_0_, ...), custom_call_target="tpu_custom_call" | custom-call | flops 7000000000 | tf_op jit(solution)/shard_map/pallas_call | solution.py:524
  31.5 6.4 %all-to-all-start = ((bf16[8,208,512]{2,1,0:T(8,128)(2,1)}), bf16[8,208,512]{2,1,0:T(8,128)(2,1)S(1)}, u32[]{:S(2)}, u32[]{:S(2)}) async-start(bf16[8,208,512]{2,1,0:T(8,128)(2,1)} %bitcast.12), calls=%async_computation | async-start | bytes 3407872 | tf_op jit(solution)/shard_map/all_to_all | solution.py:681
  38.6 4.3 %collective-permute-done.13.refs_6_ = bf16[512,512]{1,0:T(8,128)(2,1)} collective-permute-done((bf16[512,512]{1,0:T(8,128)(2,1)}, bf16[512,512]{1,0:T(8,128)(2,1)}, u32[]{:S(2)}, u32[]{:S(2)}) %collective-permute-start.13) | collective-permute-done | bytes 524320 | tf_op jit(solution)/shard_map/ppermute | solution.py:543
  46.9 4.4 %shard_map.188.x_ref = f32[416,512]{1,0:T(8,128)S(1)} custom-call(s32[2]{0:T(128)S(1)} %pad_add_fusion.pos_ref, f32[416,512]{1,0:T(8,128)S(1)} %copy-done.74, f32[1,512]{1,0:T(1,128)S(1)} %get-tuple-element.238.gain_ref, bf16[128,2048]{1,0:T(8,128)(2,1)S(1)} %copy-done.17, bf16[128,2048]{1,0:T(8,128)(2,1)S(1)} %collective-permute-done.9.refs_1_, ...), custom_call_target="tpu_custom_call" | custom-call | flops 6499999744 | tf_op jit(solution)/shard_map/pallas_call | solution.py:524
  56.5 3.9 %collective-permute-done.19.refs_6_ = bf16[128,512]{1,0:T(8,128)(2,1)S(1)} collective-permute-done((bf16[128,512]{1,0:T(8,128)(2,1)S(1)}, bf16[128,512]{1,0:T(8,128)(2,1)S(1)}, u32[]{:S(2)}, u32[]{:S(2)}) %collective-permute-start.19) | collective-permute-done | bytes 131104 | tf_op jit(solution)/shard_map/ppermute | solution.py:543
  61.8 5.6 %shard_map.189 = (f32[416,512]{1,0:T(8,128)S(1)}, bf16[416,1536]{1,0:T(8,128)(2,1)S(1)}, bf16[416,512]{1,0:T(8,128)(2,1)S(1)}) custom-call(s32[2]{0:T(128)S(1)} %pad_add_fusion.pos_ref, f32[416,512]{1,0:T(8,128)S(1)} %shard_map.188.x_ref, f32[1,512]{1,0:T(1,128)S(1)} %get-tuple-element.237.gain_ref, bf16[128,1536]{1,0:T(8,128)(2,1)S(1)} %get-tuple-element.126.refs_0_, ...), custom_call_target="tpu_custom_call" | custom-call | flops 7000000000 | tf_op jit(solution)/shard_map/pallas_call | solution.py:524
  68.6 3.9 %shard_map.191 = (bf16[416,512]{1,0:T(8,128)(2,1)S(1)}, f32[8,416]{1,0:T(8,128)S(1)}, bf16[208,512]{1,0:T(8,128)(2,1)}, bf16[208,512]{1,0:T(8,128)(2,1)}, bf16[2...) custom-call(s32[2]{0:T(128)S(1)} %pad_add_fusion.pos_ref, ...), custom_call_target="tpu_custom_call" | custom-call | flops 4600000000 | tf_op jit(solution)/shard_map/pallas_call | solution.py:524
  85.8 9.8 %shard_map.192 = (bf16[208,512]{1,0:T(8,128)(2,1)}, bf16[208,512]{1,0:T(8,128)(2,1)}, bf16[208,512]{1,0:T(8,128)(2,1)}, bf16[208,512]{1,0:T(8,128)(2,1)}, bf16[4...) custom-call(s32[2]{0:T(128)} %copy-done.47, bf16[512,2048]{1,0:T(8,128)(2,1)} %bitcast.34, ...), custom_call_target="tpu_custom_call" | custom-call | flops 8000000000 | tf_op jit(solution)/shard_map/pallas_call | solution.py:721
  100.4 7.6 %shard_map.193 = (bf16[208,512]{1,0:T(8,128)(2,1)}, bf16[208,512]{1,0:T(8,128)(2,1)}, bf16[208,512]{1,0:T(8,128)(2,1)}, bf16[208,512]{1,0:T(8,128)(2,1)}, bf16[4...) custom-call(s32[2]{0:T(128)S(1)} %copy-done.48, bf16[512,2048]{1,0:T(8,128)(2,1)S(1)} %bitcast.35, ...), custom_call_target="tpu_custom_call" | custom-call | flops 8000000000 | tf_op jit(solution)/shard_map/pallas_call | solution.py:721
  111.0 8.6 %shard_map.194 = (bf16[208,512]{1,0:T(8,128)(2,1)}, bf16[208,512]{1,0:T(8,128)(2,1)}, bf16[208,512]{1,0:T(8,128)(2,1)}, bf16[208,512]{1,0:T(8,128)(2,1)}, bf16[4...) custom-call(s32[2]{0:T(128)S(1)} %copy-done.48, bf16[512,2048]{1,0:T(8,128)(2,1)S(1)} %bitcast.36, ...), custom_call_target="tpu_custom_call" | custom-call | flops 8000000000 | tf_op jit(solution)/shard_map/pallas_call | solution.py:721
  119.6 4.2 %collective-permute-start.31 = (bf16[208,512]{1,0:T(8,128)(2,1)}, bf16[208,512]{1,0:T(8,128)(2,1)S(1)}, u32[]{:S(2)}, u32[]{:S(2)}) collective-permute-start(bf16[208,512]{1,0:T(8,128)(2,1)} %get-tuple-element.181), channel_id=1, source_target_pairs={{0,16},{4,20},{8,24},{12,28},{16,0},{20,4},{24,8},{28,12},{1,17},{... | collective-permute-start | bytes 638984 | tf_op jit(solution)/shard_map/ppermute | solution.py:543
  124.5 9.2 %shard_map.195 = (bf16[208,512]{1,0:T(8,128)(2,1)}, bf16[208,512]{1,0:T(8,128)(2,1)}, bf16[208,512]{1,0:T(8,128)(2,1)}, bf16[208,512]{1,0:T(8,128)(2,1)}, bf16[4...) custom-call(s32[2]{0:T(128)S(1)} %copy-done.48, bf16[512,2048]{1,0:T(8,128)(2,1)S(1)} %bitcast.37, ...), custom_call_target="tpu_custom_call" | custom-call | flops 8000000000 | tf_op jit(solution)/shard_map/pallas_call | solution.py:721
  141.8 12.5 %shard_map.197 = (bf16[512,2048]{1,0:T(8,128)(2,1)}, bf16[512,2048]{1,0:T(8,128)(2,1)}) custom-call(s32[2]{0:T(128)S(1)} %copy-done.48, bf16[208,512]{1,0:T(8,128)(2,1)S(1)} %copy-done.84, bf16[208,512]{1,0:T(8,128)(2,1)S(1)} %copy-done.38, bf16[208,512]{1,0:T(8,128)(2,1)S(1)} %collective-permute-done.22.refs_2_, ...), custom_call_target="tpu_custom_call" | custom-call | flops 10000000000 | tf_op jit(solution)/shard_map/pallas_call | solution.py:757
  161.4 6.3 %all-to-all-start.1 = ((bf16[8,208,512]{2,1,0:T(8,128)(2,1)}), bf16[8,208,512]{2,1,0:T(8,128)(2,1)S(1)}, u32[]{:S(2)}, u32[]{:S(2)}) async-start(bf16[8,208,512]{2,1,0:T(8,128)(2,1)} %shard_map.196), calls=%async_computation.1 | async-start | bytes 3407872 | tf_op jit(solution)/shard_map/all_to_all | solution.py:778
  174.4 12.5 %shard_map.201 = (f32[416,512]{1,0:T(8,128)}, f32[1,512]{1,0:T(1,128)}, bf16[2,2,64,2048]{3,2,1,0:T(8,128)(2,1)}, bf16[2,2,64,2048]{3,2,1,0:T(8,128)(2,1)}) custom-call(s32[2]{0:T(128)} %copy-done.47, f32[416,512]{1,0:T(8,128)} %copy-done.75, f32[1,512]{1,0:T(1,128)} %copy-done.11, bf16[416,1536]{1,0:T(8,128)(2,1)} %copy-done.76, ...), custom_call_target="tpu_custom_call" | custom-call | flops 12499999744 | tf_op jit(solution)/shard_map/pallas_call | solution.py:524
  186.9 12.1 %shard_map.202 = (f32[416,512]{1,0:T(8,128)}, f32[1,512]{1,0:T(1,128)}, bf16[2,2,128,2048]{3,2,1,0:T(8,128)(2,1)}, bf16[2,2,128,2048]{3,2,1,0:T(8,128)(2,1)}) custom-call(s32[2]{0:T(128)} %copy-done.47, f32[416,512]{1,0:T(8,128)} %copy-done.73, f32[1,512]{1,0:T(1,128)} %copy-done.10, f32[416,512]{1,0:T(8,128)} %get-tuple-element.200.dz_ref, ...), custom_call_target="tpu_custom_call" | custom-call | flops 12499999744 | tf_op jit(solution)/shard_map/pallas_call | solution.py:524
  201.1 4.8 %collective-permute-done.38.refs_2_ = bf16[2,2,64,2048]{3,2,1,0:T(8,128)(2,1)S(1)} collective-permute-done((bf16[2,2,64,2048]{3,2,1,0:T(8,128)(2,1)S(1)}, bf16[2,2,64,2048]{3,2,1,0:T(8,128)(2,1)S(1)}, u32[]{:S(2)}, u32[]{:S(2)}) %collective-permute-start.38) | collective-permute-done | bytes 1048608 | tf_op jit(solution)/shard_map/ppermute | solution.py:543
  212.2 5.2 %all-to-all-start.2 = ((bf16[8,96,2048]{2,1,0:T(8,128)(2,1)}), bf16[8,96,2048]{2,1,0:T(8,128)(2,1)S(1)}, u32[]{:S(2)}, u32[]{:S(2)}) async-start(bf16[8,96,2048]{2,1,0:T(8,128)(2,1)} %shard_map.203), calls=%async_computation.2 | async-start | bytes 6291456 | tf_op jit(solution)/shard_map/all_to_all | solution.py:577
  217.4 12.9 %shard_map.204 = (f32[416,512]{1,0:T(8,128)}, f32[1,512]{1,0:T(1,128)}, bf16[2,2,64,2176]{3,2,1,0:T(8,128)(2,1)}, bf16[2,2,64,2176]{3,2,1,0:T(8,128)(2,1)}) custom-call(s32[2]{0:T(128)} %copy-done.47, bf16[416,512]{1,0:T(8,128)(2,1)} %bitcast.28, f32[1,512]{1,0:T(1,128)} %copy-done.9, bf16[416,1536]{1,0:T(8,128)(2,1)} %copy-done.77, ...), custom_call_target="tpu_custom_call" | custom-call | flops 12499999744 | tf_op jit(solution)/shard_map/pallas_call | solution.py:524
  243.1 15.9 %all-to-all-done.2.a_ref = bf16[8,96,2048]{2,1,0:T(8,128)(2,1)S(1)} async-done(((bf16[8,96,2048]{2,1,0:T(8,128)(2,1)}), bf16[8,96,2048]{2,1,0:T(8,128)(2,1)S(1)}, u32[]{:S(2)}, u32[]{:S(2)}) %all-to-all-start.2) | async-done | bytes 3145760 | tf_op jit(solution)/shard_map/all_to_all | solution.py:577
  260.2 4.6 %all-to-all-start.3 = ((bf16[8,32,2176]{2,1,0:T(8,128)(2,1)}), bf16[8,32,2176]{2,1,0:T(8,128)(2,1)S(1)}, u32[]{:S(2)}, u32[]{:S(2)}) async-start(bf16[8,32,2176]{2,1,0:T(8,128)(2,1)} %shard_map.205), calls=%async_computation.3 | async-start | bytes 2228224 | tf_op jit(solution)/shard_map/all_to_all | solution.py:577
  272.9 12.7 %collective-permute-done.41.refs_1_ = bf16[96,2048]{1,0:T(8,128)(2,1)S(1)} collective-permute-done((bf16[96,2048]{1,0:T(8,128)(2,1)S(1)}, bf16[96,2048]{1,0:T(8,128)(2,1)S(1)}, u32[]{:S(2)}, u32[]{:S(2)}) %collective-permute-start.41) | collective-permute-done | bytes 393248 | tf_op jit(solution)/shard_map/ppermute | solution.py:543
  295.9 17.2 %collective-permute-done.43.refs_1_ = bf16[32,2176]{1,0:T(8,128)(2,1)S(1)} collective-permute-done((bf16[32,2176]{1,0:T(8,128)(2,1)S(1)}, bf16[32,2176]{1,0:T(8,128)(2,1)S(1)}, u32[]{:S(2)}, u32[]{:S(2)}) %collective-permute-start.43) | collective-permute-done | bytes 139296 | tf_op jit(solution)/shard_map/ppermute | solution.py:543
  (328 shorter events, 133.7 us)
Async XLA Ops:
  17.0 21.5 %collective-permute-start.10 = (bf16[128,2048]{1,0:T(8,128)(2,1)S(1)}, bf16[128,2048]{1,0:T(8,128)(2,1)}, u32[]{:S(2)}, u32[]{:S(2)}) collective-permute-start(bf16[128,2048]{1,0:T(8,128)(2,1)S(1)} %copy-done.17), channel_id=1, source_target_pairs={{0,2},{1,3},{2,0},{3,1},{4,6},{5,7},{6,4},{7,5},{8,10},{9,11},{10,... | collective-permute-start | bytes 1572872 | tf_op jit(solution)/shard_map/ppermute | solution.py:543
  19.1 23.8 %collective-permute-start.13 = (bf16[512,512]{1,0:T(8,128)(2,1)}, bf16[512,512]{1,0:T(8,128)(2,1)}, u32[]{:S(2)}, u32[]{:S(2)}) collective-permute-start(bf16[512,512]{1,0:T(8,128)(2,1)} %refs_4_.3), channel_id=1, source_target_pairs={{0,2},{1,3},{2,0},{3,1},{4,6},{5,7},{6,4},{7,5},{8,10},{9,11},{10,... | collective-permute-start | bytes 1572872 | tf_op jit(solution)/shard_map/ppermute | solution.py:543
  31.5 53.1 %all-to-all-start = ((bf16[8,208,512]{2,1,0:T(8,128)(2,1)}), bf16[8,208,512]{2,1,0:T(8,128)(2,1)S(1)}, u32[]{:S(2)}, u32[]{:S(2)}) async-start(bf16[8,208,512]{2,1,0:T(8,128)(2,1)} %bitcast.12), calls=%async_computation | async-start | bytes 3407872 | tf_op jit(solution)/shard_map/all_to_all | solution.py:681
  75.0 20.5 %collective-permute-start.22 = (bf16[208,512]{1,0:T(8,128)(2,1)}, bf16[208,512]{1,0:T(8,128)(2,1)S(1)}, u32[]{:S(2)}, u32[]{:S(2)}) collective-permute-start(bf16[208,512]{1,0:T(8,128)(2,1)} %get-tuple-element.139), channel_id=1, source_target_pairs={{0,8},{4,12},{8,0},{12,4},{16,24},{20,28},{24,16},{28,20},{1,9},{5... | collective-permute-start | bytes 638984 | tf_op jit(solution)/shard_map/ppermute | solution.py:543
  76.7 20.1 %collective-permute-start.23 = (bf16[208,512]{1,0:T(8,128)(2,1)}, bf16[208,512]{1,0:T(8,128)(2,1)S(1)}, u32[]{:S(2)}, u32[]{:S(2)}) collective-permute-start(bf16[208,512]{1,0:T(8,128)(2,1)} %get-tuple-element.140), channel_id=1, source_target_pairs={{0,12},{4,8},{8,4},{12,0},{16,28},{20,24},{24,20},{28,16},{1,13},{... | collective-permute-start | bytes 638984 | tf_op jit(solution)/shard_map/ppermute | solution.py:543
  76.9 31.1 %collective-permute-start.24 = (bf16[208,512]{1,0:T(8,128)(2,1)}, bf16[208,512]{1,0:T(8,128)(2,1)S(1)}, u32[]{:S(2)}, u32[]{:S(2)}) collective-permute-start(bf16[208,512]{1,0:T(8,128)(2,1)} %get-tuple-element.143), channel_id=1, source_target_pairs={{0,16},{4,20},{8,24},{12,28},{16,0},{20,4},{24,8},{28,12},{1,17},{... | collective-permute-start | bytes 638984 | tf_op jit(solution)/shard_map/ppermute | solution.py:543
  79.7 31.3 %collective-permute-start.26 = (bf16[208,512]{1,0:T(8,128)(2,1)}, bf16[208,512]{1,0:T(8,128)(2,1)}, u32[]{:S(2)}, u32[]{:S(2)}) collective-permute-start(bf16[208,512]{1,0:T(8,128)(2,1)} %get-tuple-element.147), channel_id=1, source_target_pairs={{0,20},{4,16},{8,28},{12,24},{16,4},{20,0},{24,12},{28,8},{1,21},{... | collective-permute-start | bytes 638984 | tf_op jit(solution)/shard_map/ppermute | solution.py:543
  81.0 38.6 %collective-permute-start.27 = (bf16[208,512]{1,0:T(8,128)(2,1)}, bf16[208,512]{1,0:T(8,128)(2,1)}, u32[]{:S(2)}, u32[]{:S(2)}) collective-permute-start(bf16[208,512]{1,0:T(8,128)(2,1)} %get-tuple-element.150), channel_id=1, source_target_pairs={{0,24},{4,28},{8,16},{12,20},{16,8},{20,12},{24,0},{28,4},{1,25},{... | collective-permute-start | bytes 638984 | tf_op jit(solution)/shard_map/ppermute | solution.py:543
  95.6 29.0 %collective-permute-start.30 = (bf16[208,512]{1,0:T(8,128)(2,1)S(1)}, bf16[208,512]{1,0:T(8,128)(2,1)S(1)}, u32[]{:S(2)}, u32[]{:S(2)}) collective-permute-start(bf16[208,512]{1,0:T(8,128)(2,1)S(1)} %copy-done.94), channel_id=1, source_target_pairs={{0,28},{4,24},{8,20},{12,16},{16,12},{20,8},{24,4},{28,0},{1,29},{... | collective-permute-start | bytes 638984 | tf_op jit(solution)/shard_map/ppermute | solution.py:543
  119.6 36.7 %collective-permute-start.31 = (bf16[208,512]{1,0:T(8,128)(2,1)}, bf16[208,512]{1,0:T(8,128)(2,1)S(1)}, u32[]{:S(2)}, u32[]{:S(2)}) collective-permute-start(bf16[208,512]{1,0:T(8,128)(2,1)} %get-tuple-element.181), channel_id=1, source_target_pairs={{0,16},{4,20},{8,24},{12,28},{16,0},{20,4},{24,8},{28,12},{1,17},{... | collective-permute-start | bytes 638984 | tf_op jit(solution)/shard_map/ppermute | solution.py:543
  123.8 32.4 %collective-permute-start.32 = (bf16[208,512]{1,0:T(8,128)(2,1)}, bf16[208,512]{1,0:T(8,128)(2,1)S(1)}, u32[]{:S(2)}, u32[]{:S(2)}) collective-permute-start(bf16[208,512]{1,0:T(8,128)(2,1)} %get-tuple-element.182), channel_id=1, source_target_pairs={{0,20},{4,16},{8,28},{12,24},{16,4},{20,0},{24,12},{28,8},{1,21},{... | collective-permute-start | bytes 638984 | tf_op jit(solution)/shard_map/ppermute | solution.py:543
  133.7 22.5 %collective-permute-start.33 = (bf16[208,512]{1,0:T(8,128)(2,1)}, bf16[208,512]{1,0:T(8,128)(2,1)S(1)}, u32[]{:S(2)}, u32[]{:S(2)}) collective-permute-start(bf16[208,512]{1,0:T(8,128)(2,1)} %get-tuple-element.183), channel_id=1, source_target_pairs={{0,24},{4,28},{8,16},{12,20},{16,8},{20,12},{24,0},{28,4},{1,25},{... | collective-permute-start | bytes 638984 | tf_op jit(solution)/shard_map/ppermute | solution.py:543
  134.9 21.4 %collective-permute-start.34 = (bf16[208,512]{1,0:T(8,128)(2,1)}, bf16[208,512]{1,0:T(8,128)(2,1)S(1)}, u32[]{:S(2)}, u32[]{:S(2)}) collective-permute-start(bf16[208,512]{1,0:T(8,128)(2,1)} %get-tuple-element.184), channel_id=1, source_target_pairs={{0,28},{4,24},{8,20},{12,16},{16,12},{20,8},{24,4},{28,0},{1,29},{... | collective-permute-start | bytes 638984 | tf_op jit(solution)/shard_map/ppermute | solution.py:543
  161.4 49.7 %all-to-all-start.1 = ((bf16[8,208,512]{2,1,0:T(8,128)(2,1)}), bf16[8,208,512]{2,1,0:T(8,128)(2,1)S(1)}, u32[]{:S(2)}, u32[]{:S(2)}) async-start(bf16[8,208,512]{2,1,0:T(8,128)(2,1)} %shard_map.196), calls=%async_computation.1 | async-start | bytes 3407872 | tf_op jit(solution)/shard_map/all_to_all | solution.py:778
  172.3 26.7 %collective-permute-start.36 = (bf16[128,2048]{1,0:T(8,128)(2,1)}, bf16[128,2048]{1,0:T(8,128)(2,1)S(1)}, u32[]{:S(2)}, u32[]{:S(2)}) collective-permute-start(bf16[128,2048]{1,0:T(8,128)(2,1)} %get-tuple-element.221.refs_0_), channel_id=1, source_target_pairs={{0,2},{1,3},{2,0},{3,1},{4,6},{5,7},{6,4},{7,5},{8,10},{9,11},{10,... | collective-permute-start | bytes 1572872 | tf_op jit(solution)/shard_map/ppermute | solution.py:543
  173.9 26.0 %collective-permute-start.37 = (bf16[128,2048]{1,0:T(8,128)(2,1)}, bf16[128,2048]{1,0:T(8,128)(2,1)S(1)}, u32[]{:S(2)}, u32[]{:S(2)}) collective-permute-start(bf16[128,2048]{1,0:T(8,128)(2,1)} %get-tuple-element.197.refs_1_), channel_id=1, source_target_pairs={{0,2},{1,3},{2,0},{3,1},{4,6},{5,7},{6,4},{7,5},{8,10},{9,11},{10,... | collective-permute-start | bytes 1572872 | tf_op jit(solution)/shard_map/ppermute | solution.py:543
  212.2 46.8 %all-to-all-start.2 = ((bf16[8,96,2048]{2,1,0:T(8,128)(2,1)}), bf16[8,96,2048]{2,1,0:T(8,128)(2,1)S(1)}, u32[]{:S(2)}, u32[]{:S(2)}) async-start(bf16[8,96,2048]{2,1,0:T(8,128)(2,1)} %shard_map.203), calls=%async_computation.2 | async-start | bytes 6291456 | tf_op jit(solution)/shard_map/all_to_all | solution.py:577
  260.2 28.3 %all-to-all-start.3 = ((bf16[8,32,2176]{2,1,0:T(8,128)(2,1)}), bf16[8,32,2176]{2,1,0:T(8,128)(2,1)S(1)}, u32[]{:S(2)}, u32[]{:S(2)}) async-start(bf16[8,32,2176]{2,1,0:T(8,128)(2,1)} %shard_map.205), calls=%async_computation.3 | async-start | bytes 2228224 | tf_op jit(solution)/shard_map/all_to_all | solution.py:577
  266.0 19.6 %collective-permute-start.41 = (bf16[96,2048]{1,0:T(8,128)(2,1)S(1)}, bf16[96,2048]{1,0:T(8,128)(2,1)S(1)}, u32[]{:S(2)}, u32[]{:S(2)}) collective-permute-start(bf16[96,2048]{1,0:T(8,128)(2,1)S(1)} %copy-done.35), channel_id=1, source_target_pairs={{0,16},{4,20},{8,24},{12,28},{16,0},{20,4},{24,8},{28,12},{1,17},{... | collective-permute-start | bytes 1179656 | tf_op jit(solution)/shard_map/ppermute | solution.py:543
  289.2 25.1 %collective-permute-start.50 = (bf16[256,2048]{1,0:T(8,128)(2,1)S(1)}, bf16[256,2048]{1,0:T(8,128)(2,1)S(1)}, u32[]{:S(2)}, u32[]{:S(2)}) collective-permute-start(bf16[256,2048]{1,0:T(8,128)(2,1)S(1)} %copy-done.14), channel_id=1, source_target_pairs={{0,2},{1,3},{2,0},{3,1},{4,6},{5,7},{6,4},{7,5},{8,10},{9,11},{10,... | collective-permute-start | bytes 3145736 | tf_op jit(solution)/shard_map/ppermute | solution.py:543
  290.8 23.1 %collective-permute-start.47 = (bf16[96,2048]{1,0:T(8,128)(2,1)}, bf16[96,2048]{1,0:T(8,128)(2,1)S(1)}, u32[]{:S(2)}, u32[]{:S(2)}) collective-permute-start(bf16[96,2048]{1,0:T(8,128)(2,1)} %shard_map.211.refs_4_.refs_0_), channel_id=1, source_target_pairs={{0,4},{4,0},{8,12},{12,8},{16,20},{20,16},{24,28},{28,24},{1,5},{5... | collective-permute-start | bytes 1179656 | tf_op jit(solution)/shard_map/ppermute | solution.py:543
  292.2 21.6 %collective-permute-start.48 = (bf16[96,2048]{1,0:T(8,128)(2,1)}, bf16[96,2048]{1,0:T(8,128)(2,1)S(1)}, u32[]{:S(2)}, u32[]{:S(2)}) collective-permute-start(bf16[96,2048]{1,0:T(8,128)(2,1)} %shard_map.211.refs_4_.refs_0_), channel_id=1, source_target_pairs={{0,8},{4,12},{8,0},{12,4},{16,24},{20,28},{24,16},{28,20},{1,9},{5... | collective-permute-start | bytes 1179656 | tf_op jit(solution)/shard_map/ppermute | solution.py:543
  294.6 19.7 %collective-permute-start.49 = (bf16[96,2048]{1,0:T(8,128)(2,1)}, bf16[96,2048]{1,0:T(8,128)(2,1)S(1)}, u32[]{:S(2)}, u32[]{:S(2)}) collective-permute-start(bf16[96,2048]{1,0:T(8,128)(2,1)} %shard_map.211.refs_4_.refs_0_), channel_id=1, source_target_pairs={{0,12},{4,8},{8,4},{12,0},{16,28},{20,24},{24,20},{28,16},{1,13},{... | collective-permute-start | bytes 1179656 | tf_op jit(solution)/shard_map/ppermute | solution.py:543
  294.7 18.5 %collective-permute-start.43 = (bf16[32,2176]{1,0:T(8,128)(2,1)S(1)}, bf16[32,2176]{1,0:T(8,128)(2,1)S(1)}, u32[]{:S(2)}, u32[]{:S(2)}) collective-permute-start(bf16[32,2176]{1,0:T(8,128)(2,1)S(1)} %copy-done.40), channel_id=1, source_target_pairs={{0,16},{4,20},{8,24},{12,28},{16,0},{20,4},{24,8},{28,12},{1,17},{... | collective-permute-start | bytes 417800 | tf_op jit(solution)/shard_map/ppermute | solution.py:543
  (127 other events, 1127.4 us)

commit v3 on v2

--- a/solution.py
+++ b/solution.py
@@ -764,7 +764,7 @@
         out_specs=[pl.BlockSpec((512, 1024), lambda j: (0, j))] * 2,
         out_shape=[pltpu.HBM((512, FF), BF16)] * 2,
         cost_estimate=spent(10.0),
-        compiler_params=pltpu.CompilerParams(vmem_limit_bytes=VMEM_LIMIT),
+        compiler_params=pltpu.CompilerParams(vmem_limit_bytes=58 * 1024 * 1024),
     )(pos, *c_in, *fs, *dhs, *dys)
     x3_late, z_block, grad_send, grad_keep = lax.optimization_barrier((x3, z_block, grad_send, grad_keep))
     g3, gain3, drouter = call(
@@ -827,8 +827,10 @@
         mlp1, mlp2 = call(
             finish_mlp_kernel,
             [((D // 4, FF), F32), ((4, 128, D), F32)],
-            pos, *bulk, specs=[SCALAR] + [WHOLE] * 4, us=2.0,
+            pos, after(bulk[0], tail[1]), *bulk[1:], specs=[SCALAR] + [WHOLE] * 4, us=2.0,
         )
+        expert2 = join(join_columns_kernel, (FF, D), grads[2:], [last])
+        tail[0] = after(tail[0], expert2)
         grad_in, grad_out, smalls = call(
             finish_attention_kernel,
             [((2, D // 4, 3 * D), F32), ((2, D // 4, D), F32), (((wide - 4 * D) // 128 * STRIP, 128), F32)],
@@ -837,6 +839,7 @@
         mlp2 = mlp2.reshape(FF // 4, D)
     else:
         last = flip(grads[2], "wshard", 2)
+        expert2 = join(join_columns_kernel, (FF, D), grads[2:], [last])
         first, second, mlp = sum_plainly(*first), sum_plainly(*second), sum_plainly(*mlp)
         grad_in = jnp.stack([first[:, : 3 * D], second[:, : 3 * D]])
         grad_out = jnp.stack([first[:, 3 * D : 4 * D], second[:, 3 * D :]])
@@ -845,7 +848,6 @@
         final_rows, input_grad = contract(final, pictures), contract(dx, pictures)
         mlp2 = jnp.stack([mlp[64:128], mlp[192:256]]).reshape(2, 64, 4, D).transpose(2, 0, 1, 3).reshape(FF // 4, D)
 
-    expert2 = join(join_columns_kernel, (FF, D), grads[2:], [last])
     return (
         final_rows,
         input_grad,

time: 339 us -> 335 us (0.988)
  local copies, waits for them, and re-layouts: 36.8 us -> 32.2 us
    unnamed x190 -> x176, local copies, waits for them, and re-layouts: 26 us -> 21.5 us
  transfers between devices with their start and end apart: 56 -> 56, of which waited for: 19 -> 17; matrix products, arithmetic and copies ran while one was open for 3% -> 3% of each run, Pallas kernels for 39% -> 40%
where the time goes in v3:
time: 335 us; the launch traced here: 329 us
  Pallas kernels  140 us (42%)
  waiting for transfers between devices  77.8 us (23%)
  starting transfers between devices  77.1 us (23%)
  local copies, waits for them, and re-layouts  32.2 us (10%)
    pallas_call x25, Pallas kernels, call(): pl.pallas_call(kernel, out_shape=[(pltpu.HBM if rest else jax.ShapeDtypeS...  89.8 us
    ppermute x52, waiting for transfers between devices, flip(): lax.ppermute(array, axis, [(i, i ^ bit) for i in range(lax.axis_size(axis...  59.1 us
    ppermute x52, starting transfers between devices, flip(): lax.ppermute(array, axis, [(i, i ^ bit) for i in range(lax.axis_size(axis...  52.7 us
    pallas_call x4, Pallas kernels, local(): pl.pallas_call(functools.partial(experts_kernel, slots, per, each), out_s...  34.5 us
    unnamed x176, local copies, waits for them, and re-layouts  21.5 us
    all_to_all x2, waiting for transfers between devices, trade_cube(): lax.all_to_all(blocks, ('expert', 'wshard'), 0, 0, axis_index_groups=grou...  18.7 us
    pallas_call x1, Pallas kernels, local(): pl.pallas_call(functools.partial(expert_grads_kernel, n), grid=(FF // 102...  15.3 us
    all_to_all x2, starting transfers between devices, trade_cube(): lax.all_to_all(blocks, ('expert', 'wshard'), 0, 0, axis_index_groups=grou...  9.75 us
  transfers between devices with their start and end apart: 56, of which 17 were waited for; matrix products, arithmetic and copies ran while one was open for 3% of the time, Pallas kernels for 40%

profile of v3, /device:TPU:0, one launch (start us, length us, event | category | flops | bytes accessed | tf_op | source)
XLA Modules:
  0.0 329.5 jit_solution(7015661850773965151)
XLA Ops:
  8.0 7.0 %collective-permute-done.1.refs_2_ = bf16[16,128]{1,0:T(8,128)(2,1)S(1)} collective-permute-done((bf16[16,128]{1,0:T(8,128)(2,1)S(1)}, bf16[16,128]{1,0:T(8,128)(2,1)S(1)}, u32[]{:S(2)}, u32[]{:S(2)}) %collective-permute-start.1) | collective-permute-done | bytes 4128 | tf_op jit(solution)/shard_map/ppermute | solution.py:543
  19.3 5.6 %shard_map.187 = (f32[416,512]{1,0:T(8,128)S(1)}, bf16[416,1536]{1,0:T(8,128)(2,1)S(1)}, bf16[416,512]{1,0:T(8,128)(2,1)S(1)}) custom-call(s32[2]{0:T(128)S(1)} %pad_add_fusion.pos_ref, bf16[416,512]{1,0:T(8,128)(2,1)S(1)} %bitcast.27, f32[1,512]{1,0:T(1,128)S(1)} %get-tuple-element.243.gain_ref, bf16[128,1536]{1,0:T(8,128)(2,1)S(1)} %get-tuple-element.237.refs_0_, ...), custom_call_target="tpu_custom_call" | custom-call | flops 7000000000 | tf_op jit(solution)/shard_map/pallas_call | solution.py:524
  31.4 6.4 %all-to-all-start = ((bf16[8,208,512]{2,1,0:T(8,128)(2,1)}), bf16[8,208,512]{2,1,0:T(8,128)(2,1)S(1)}, u32[]{:S(2)}, u32[]{:S(2)}) async-start(bf16[8,208,512]{2,1,0:T(8,128)(2,1)} %bitcast.12), calls=%async_computation | async-start | bytes 3407872 | tf_op jit(solution)/shard_map/all_to_all | solution.py:681
  38.5 4.4 %collective-permute-done.13.refs_6_ = bf16[512,512]{1,0:T(8,128)(2,1)} collective-permute-done((bf16[512,512]{1,0:T(8,128)(2,1)}, bf16[512,512]{1,0:T(8,128)(2,1)}, u32[]{:S(2)}, u32[]{:S(2)}) %collective-permute-start.13) | collective-permute-done | bytes 524320 | tf_op jit(solution)/shard_map/ppermute | solution.py:543
  46.9 4.4 %shard_map.188.x_ref = f32[416,512]{1,0:T(8,128)S(1)} custom-call(s32[2]{0:T(128)S(1)} %pad_add_fusion.pos_ref, f32[416,512]{1,0:T(8,128)S(1)} %copy-done.71, f32[1,512]{1,0:T(1,128)S(1)} %get-tuple-element.242.gain_ref, bf16[128,2048]{1,0:T(8,128)(2,1)S(1)} %copy-done.17, bf16[128,2048]{1,0:T(8,128)(2,1)S(1)} %collective-permute-done.9.refs_1_, ...), custom_call_target="tpu_custom_call" | custom-call | flops 6499999744 | tf_op jit(solution)/shard_map/pallas_call | solution.py:524
  56.5 3.9 %collective-permute-done.19.refs_6_ = bf16[128,512]{1,0:T(8,128)(2,1)S(1)} collective-permute-done((bf16[128,512]{1,0:T(8,128)(2,1)S(1)}, bf16[128,512]{1,0:T(8,128)(2,1)S(1)}, u32[]{:S(2)}, u32[]{:S(2)}) %collective-permute-start.19) | collective-permute-done | bytes 131104 | tf_op jit(solution)/shard_map/ppermute | solution.py:543
  61.8 5.6 %shard_map.189 = (f32[416,512]{1,0:T(8,128)S(1)}, bf16[416,1536]{1,0:T(8,128)(2,1)S(1)}, bf16[416,512]{1,0:T(8,128)(2,1)S(1)}) custom-call(s32[2]{0:T(128)S(1)} %pad_add_fusion.pos_ref, f32[416,512]{1,0:T(8,128)S(1)} %shard_map.188.x_ref, f32[1,512]{1,0:T(1,128)S(1)} %get-tuple-element.241.gain_ref, bf16[128,1536]{1,0:T(8,128)(2,1)S(1)} %get-tuple-element.128.refs_0_, ...), custom_call_target="tpu_custom_call" | custom-call | flops 7000000000 | tf_op jit(solution)/shard_map/pallas_call | solution.py:524
  68.6 3.9 %shard_map.191 = (bf16[416,512]{1,0:T(8,128)(2,1)S(1)}, f32[8,416]{1,0:T(8,128)S(1)}, bf16[208,512]{1,0:T(8,128)(2,1)}, bf16[208,512]{1,0:T(8,128)(2,1)}, bf16[2...) custom-call(s32[2]{0:T(128)S(1)} %pad_add_fusion.pos_ref, ...), custom_call_target="tpu_custom_call" | custom-call | flops 4600000000 | tf_op jit(solution)/shard_map/pallas_call | solution.py:524
  85.8 9.8 %shard_map.192 = (bf16[208,512]{1,0:T(8,128)(2,1)}, bf16[208,512]{1,0:T(8,128)(2,1)}, bf16[208,512]{1,0:T(8,128)(2,1)}, bf16[208,512]{1,0:T(8,128)(2,1)}, bf16[4...) custom-call(s32[2]{0:T(128)} %copy-done.49, bf16[512,2048]{1,0:T(8,128)(2,1)} %bitcast.34, ...), custom_call_target="tpu_custom_call" | custom-call | flops 8000000000 | tf_op jit(solution)/shard_map/pallas_call | solution.py:721
  100.4 7.6 %shard_map.193 = (bf16[208,512]{1,0:T(8,128)(2,1)}, bf16[208,512]{1,0:T(8,128)(2,1)}, bf16[208,512]{1,0:T(8,128)(2,1)}, bf16[208,512]{1,0:T(8,128)(2,1)}, bf16[4...) custom-call(s32[2]{0:T(128)S(1)} %copy-done.50, bf16[512,2048]{1,0:T(8,128)(2,1)S(1)} %bitcast.35, ...), custom_call_target="tpu_custom_call" | custom-call | flops 8000000000 | tf_op jit(solution)/shard_map/pallas_call | solution.py:721
  111.1 8.6 %shard_map.194 = (bf16[208,512]{1,0:T(8,128)(2,1)}, bf16[208,512]{1,0:T(8,128)(2,1)}, bf16[208,512]{1,0:T(8,128)(2,1)}, bf16[208,512]{1,0:T(8,128)(2,1)}, bf16[4...) custom-call(s32[2]{0:T(128)S(1)} %copy-done.50, bf16[512,2048]{1,0:T(8,128)(2,1)S(1)} %bitcast.36, ...), custom_call_target="tpu_custom_call" | custom-call | flops 8000000000 | tf_op jit(solution)/shard_map/pallas_call | solution.py:721
  119.7 4.2 %collective-permute-start.31 = (bf16[208,512]{1,0:T(8,128)(2,1)}, bf16[208,512]{1,0:T(8,128)(2,1)S(1)}, u32[]{:S(2)}, u32[]{:S(2)}) collective-permute-start(bf16[208,512]{1,0:T(8,128)(2,1)} %get-tuple-element.183), channel_id=1, source_target_pairs={{0,16},{4,20},{8,24},{12,28},{16,0},{20,4},{24,8},{28,12},{1,17},{... | collective-permute-start | bytes 638984 | tf_op jit(solution)/shard_map/ppermute | solution.py:543
  124.5 8.5 %shard_map.195 = (bf16[208,512]{1,0:T(8,128)(2,1)}, bf16[208,512]{1,0:T(8,128)(2,1)}, bf16[208,512]{1,0:T(8,128)(2,1)}, bf16[208,512]{1,0:T(8,128)(2,1)}, bf16[4...) custom-call(s32[2]{0:T(128)S(1)} %copy-done.50, bf16[512,2048]{1,0:T(8,128)(2,1)S(1)} %bitcast.37, ...), custom_call_target="tpu_custom_call" | custom-call | flops 8000000000 | tf_op jit(solution)/shard_map/pallas_call | solution.py:721
  137.2 15.3 %shard_map.197 = (bf16[512,2048]{1,0:T(8,128)(2,1)}, bf16[512,2048]{1,0:T(8,128)(2,1)}) custom-call(s32[2]{0:T(128)} %copy-done.49, bf16[208,512]{1,0:T(8,128)(2,1)} %get-tuple-element.137.refs_2_.refs_0_, bf16[208,512]{1,0:T(8,128)(2,1)} %copy-done.86, bf16[208,512]{1,0:T(8,128)(2,1)} %copy-done.37, bf16[208,512]{1,0:T(8,128)(2,1)} %copy-done.38, ...), custom_call_target="tpu_custom_call" | custom-call | flops 10000000000 | tf_op jit(solution)/shard_map/pallas_call | solution.py:757
  159.0 8.2 %all-to-all-start.1 = ((bf16[8,208,512]{2,1,0:T(8,128)(2,1)}), bf16[8,208,512]{2,1,0:T(8,128)(2,1)S(1)}, u32[]{:S(2)}, u32[]{:S(2)}) async-start(bf16[8,208,512]{2,1,0:T(8,128)(2,1)} %shard_map.196), calls=%async_computation.1 | async-start | bytes 3407872 | tf_op jit(solution)/shard_map/all_to_all | solution.py:778
  174.0 12.5 %shard_map.201 = (f32[416,512]{1,0:T(8,128)}, f32[1,512]{1,0:T(1,128)}, bf16[2,2,64,2048]{3,2,1,0:T(8,128)(2,1)}, bf16[2,2,64,2048]{3,2,1,0:T(8,128)(2,1)}) custom-call(s32[2]{0:T(128)} %copy-done.49, f32[416,512]{1,0:T(8,128)} %copy-done.72, f32[1,512]{1,0:T(1,128)} %copy-done.11, bf16[416,1536]{1,0:T(8,128)(2,1)} %copy-done.73, ...), custom_call_target="tpu_custom_call" | custom-call | flops 12499999744 | tf_op jit(solution)/shard_map/pallas_call | solution.py:524
  186.5 12.1 %shard_map.202 = (f32[416,512]{1,0:T(8,128)}, f32[1,512]{1,0:T(1,128)}, bf16[2,2,128,2048]{3,2,1,0:T(8,128)(2,1)}, bf16[2,2,128,2048]{3,2,1,0:T(8,128)(2,1)}) custom-call(s32[2]{0:T(128)} %copy-done.49, f32[416,512]{1,0:T(8,128)} %copy-done.70, f32[1,512]{1,0:T(1,128)} %copy-done.10, f32[416,512]{1,0:T(8,128)} %get-tuple-element.202.dz_ref, ...), custom_call_target="tpu_custom_call" | custom-call | flops 12499999744 | tf_op jit(solution)/shard_map/pallas_call | solution.py:524
  200.7 4.8 %collective-permute-done.38.refs_2_ = bf16[2,2,64,2048]{3,2,1,0:T(8,128)(2,1)S(1)} collective-permute-done((bf16[2,2,64,2048]{3,2,1,0:T(8,128)(2,1)S(1)}, bf16[2,2,64,2048]{3,2,1,0:T(8,128)(2,1)S(1)}, u32[]{:S(2)}, u32[]{:S(2)}) %collective-permute-start.38) | collective-permute-done | bytes 1048608 | tf_op jit(solution)/shard_map/ppermute | solution.py:543
  211.8 5.2 %all-to-all-start.2 = ((bf16[8,96,2048]{2,1,0:T(8,128)(2,1)}), bf16[8,96,2048]{2,1,0:T(8,128)(2,1)S(1)}, u32[]{:S(2)}, u32[]{:S(2)}) async-start(bf16[8,96,2048]{2,1,0:T(8,128)(2,1)} %shard_map.203), calls=%async_computation.2 | async-start | bytes 6291456 | tf_op jit(solution)/shard_map/all_to_all | solution.py:577
  217.0 12.8 %shard_map.204 = (f32[416,512]{1,0:T(8,128)}, f32[1,512]{1,0:T(1,128)}, bf16[2,2,64,2176]{3,2,1,0:T(8,128)(2,1)}, bf16[2,2,64,2176]{3,2,1,0:T(8,128)(2,1)}) custom-call(s32[2]{0:T(128)} %copy-done.49, bf16[416,512]{1,0:T(8,128)(2,1)} %bitcast.28, f32[1,512]{1,0:T(1,128)} %copy-done.9, bf16[416,1536]{1,0:T(8,128)(2,1)} %copy-done.74, ...), custom_call_target="tpu_custom_call" | custom-call | flops 12499999744 | tf_op jit(solution)/shard_map/pallas_call | solution.py:524
  242.7 15.9 %all-to-all-done.2.a_ref = bf16[8,96,2048]{2,1,0:T(8,128)(2,1)S(1)} async-done(((bf16[8,96,2048]{2,1,0:T(8,128)(2,1)}), bf16[8,96,2048]{2,1,0:T(8,128)(2,1)S(1)}, u32[]{:S(2)}, u32[]{:S(2)}) %all-to-all-start.2) | async-done | bytes 3145760 | tf_op jit(solution)/shard_map/all_to_all | solution.py:577
  259.7 4.6 %all-to-all-start.3 = ((bf16[8,32,2176]{2,1,0:T(8,128)(2,1)}), bf16[8,32,2176]{2,1,0:T(8,128)(2,1)S(1)}, u32[]{:S(2)}, u32[]{:S(2)}) async-start(bf16[8,32,2176]{2,1,0:T(8,128)(2,1)} %shard_map.205), calls=%async_computation.3 | async-start | bytes 2228224 | tf_op jit(solution)/shard_map/all_to_all | solution.py:577
  272.5 12.7 %collective-permute-done.41.refs_1_ = bf16[96,2048]{1,0:T(8,128)(2,1)S(1)} collective-permute-done((bf16[96,2048]{1,0:T(8,128)(2,1)S(1)}, bf16[96,2048]{1,0:T(8,128)(2,1)S(1)}, u32[]{:S(2)}, u32[]{:S(2)}) %collective-permute-start.41) | collective-permute-done | bytes 393248 | tf_op jit(solution)/shard_map/ppermute | solution.py:543
  295.5 17.2 %collective-permute-done.43.refs_1_ = bf16[32,2176]{1,0:T(8,128)(2,1)S(1)} collective-permute-done((bf16[32,2176]{1,0:T(8,128)(2,1)S(1)}, bf16[32,2176]{1,0:T(8,128)(2,1)S(1)}, u32[]{:S(2)}, u32[]{:S(2)}) %collective-permute-start.43) | collective-permute-done | bytes 139296 | tf_op jit(solution)/shard_map/ppermute | solution.py:543
  (314 shorter events, 126.4 us)
Async XLA Ops:
  17.0 21.4 %collective-permute-start.10 = (bf16[128,2048]{1,0:T(8,128)(2,1)S(1)}, bf16[128,2048]{1,0:T(8,128)(2,1)}, u32[]{:S(2)}, u32[]{:S(2)}) collective-permute-start(bf16[128,2048]{1,0:T(8,128)(2,1)S(1)} %copy-done.17), channel_id=1, source_target_pairs={{0,2},{1,3},{2,0},{3,1},{4,6},{5,7},{6,4},{7,5},{8,10},{9,11},{10,... | collective-permute-start | bytes 1572872 | tf_op jit(solution)/shard_map/ppermute | solution.py:543
  19.1 23.8 %collective-permute-start.13 = (bf16[512,512]{1,0:T(8,128)(2,1)}, bf16[512,512]{1,0:T(8,128)(2,1)}, u32[]{:S(2)}, u32[]{:S(2)}) collective-permute-start(bf16[512,512]{1,0:T(8,128)(2,1)} %refs_4_.3), channel_id=1, source_target_pairs={{0,2},{1,3},{2,0},{3,1},{4,6},{5,7},{6,4},{7,5},{8,10},{9,11},{10,... | collective-permute-start | bytes 1572872 | tf_op jit(solution)/shard_map/ppermute | solution.py:543
  31.4 53.1 %all-to-all-start = ((bf16[8,208,512]{2,1,0:T(8,128)(2,1)}), bf16[8,208,512]{2,1,0:T(8,128)(2,1)S(1)}, u32[]{:S(2)}, u32[]{:S(2)}) async-start(bf16[8,208,512]{2,1,0:T(8,128)(2,1)} %bitcast.12), calls=%async_computation | async-start | bytes 3407872 | tf_op jit(solution)/shard_map/all_to_all | solution.py:681
  75.0 20.5 %collective-permute-start.22 = (bf16[208,512]{1,0:T(8,128)(2,1)}, bf16[208,512]{1,0:T(8,128)(2,1)S(1)}, u32[]{:S(2)}, u32[]{:S(2)}) collective-permute-start(bf16[208,512]{1,0:T(8,128)(2,1)} %get-tuple-element.141), channel_id=1, source_target_pairs={{0,8},{4,12},{8,0},{12,4},{16,24},{20,28},{24,16},{28,20},{1,9},{5... | collective-permute-start | bytes 638984 | tf_op jit(solution)/shard_map/ppermute | solution.py:543
  76.7 20.1 %collective-permute-start.23 = (bf16[208,512]{1,0:T(8,128)(2,1)}, bf16[208,512]{1,0:T(8,128)(2,1)S(1)}, u32[]{:S(2)}, u32[]{:S(2)}) collective-permute-start(bf16[208,512]{1,0:T(8,128)(2,1)} %get-tuple-element.142), channel_id=1, source_target_pairs={{0,12},{4,8},{8,4},{12,0},{16,28},{20,24},{24,20},{28,16},{1,13},{... | collective-permute-start | bytes 638984 | tf_op jit(solution)/shard_map/ppermute | solution.py:543
  76.9 31.1 %collective-permute-start.24 = (bf16[208,512]{1,0:T(8,128)(2,1)}, bf16[208,512]{1,0:T(8,128)(2,1)S(1)}, u32[]{:S(2)}, u32[]{:S(2)}) collective-permute-start(bf16[208,512]{1,0:T(8,128)(2,1)} %get-tuple-element.145), channel_id=1, source_target_pairs={{0,16},{4,20},{8,24},{12,28},{16,0},{20,4},{24,8},{28,12},{1,17},{... | collective-permute-start | bytes 638984 | tf_op jit(solution)/shard_map/ppermute | solution.py:543
  79.7 31.4 %collective-permute-start.26 = (bf16[208,512]{1,0:T(8,128)(2,1)}, bf16[208,512]{1,0:T(8,128)(2,1)}, u32[]{:S(2)}, u32[]{:S(2)}) collective-permute-start(bf16[208,512]{1,0:T(8,128)(2,1)} %get-tuple-element.149), channel_id=1, source_target_pairs={{0,20},{4,16},{8,28},{12,24},{16,4},{20,0},{24,12},{28,8},{1,21},{... | collective-permute-start | bytes 638984 | tf_op jit(solution)/shard_map/ppermute | solution.py:543
  81.0 38.7 %collective-permute-start.27 = (bf16[208,512]{1,0:T(8,128)(2,1)}, bf16[208,512]{1,0:T(8,128)(2,1)}, u32[]{:S(2)}, u32[]{:S(2)}) collective-permute-start(bf16[208,512]{1,0:T(8,128)(2,1)} %get-tuple-element.152), channel_id=1, source_target_pairs={{0,24},{4,28},{8,16},{12,20},{16,8},{20,12},{24,0},{28,4},{1,25},{... | collective-permute-start | bytes 638984 | tf_op jit(solution)/shard_map/ppermute | solution.py:543
  95.6 28.9 %collective-permute-start.30 = (bf16[208,512]{1,0:T(8,128)(2,1)S(1)}, bf16[208,512]{1,0:T(8,128)(2,1)S(1)}, u32[]{:S(2)}, u32[]{:S(2)}) collective-permute-start(bf16[208,512]{1,0:T(8,128)(2,1)S(1)} %copy-done.87), channel_id=1, source_target_pairs={{0,28},{4,24},{8,20},{12,16},{16,12},{20,8},{24,4},{28,0},{1,29},{... | collective-permute-start | bytes 638984 | tf_op jit(solution)/shard_map/ppermute | solution.py:543
  119.7 34.8 %collective-permute-start.31 = (bf16[208,512]{1,0:T(8,128)(2,1)}, bf16[208,512]{1,0:T(8,128)(2,1)S(1)}, u32[]{:S(2)}, u32[]{:S(2)}) collective-permute-start(bf16[208,512]{1,0:T(8,128)(2,1)} %get-tuple-element.183), channel_id=1, source_target_pairs={{0,16},{4,20},{8,24},{12,28},{16,0},{20,4},{24,8},{28,12},{1,17},{... | collective-permute-start | bytes 638984 | tf_op jit(solution)/shard_map/ppermute | solution.py:543
  123.9 30.6 %collective-permute-start.32 = (bf16[208,512]{1,0:T(8,128)(2,1)}, bf16[208,512]{1,0:T(8,128)(2,1)S(1)}, u32[]{:S(2)}, u32[]{:S(2)}) collective-permute-start(bf16[208,512]{1,0:T(8,128)(2,1)} %get-tuple-element.184), channel_id=1, source_target_pairs={{0,20},{4,16},{8,28},{12,24},{16,4},{20,0},{24,12},{28,8},{1,21},{... | collective-permute-start | bytes 638984 | tf_op jit(solution)/shard_map/ppermute | solution.py:543
  133.0 21.5 %collective-permute-start.33 = (bf16[208,512]{1,0:T(8,128)(2,1)}, bf16[208,512]{1,0:T(8,128)(2,1)S(1)}, u32[]{:S(2)}, u32[]{:S(2)}) collective-permute-start(bf16[208,512]{1,0:T(8,128)(2,1)} %get-tuple-element.185), channel_id=1, source_target_pairs={{0,24},{4,28},{8,16},{12,20},{16,8},{20,12},{24,0},{28,4},{1,25},{... | collective-permute-start | bytes 638984 | tf_op jit(solution)/shard_map/ppermute | solution.py:543
  134.9 19.6 %collective-permute-start.34 = (bf16[208,512]{1,0:T(8,128)(2,1)}, bf16[208,512]{1,0:T(8,128)(2,1)S(1)}, u32[]{:S(2)}, u32[]{:S(2)}) collective-permute-start(bf16[208,512]{1,0:T(8,128)(2,1)} %get-tuple-element.186), channel_id=1, source_target_pairs={{0,28},{4,24},{8,20},{12,16},{16,12},{20,8},{24,4},{28,0},{1,29},{... | collective-permute-start | bytes 638984 | tf_op jit(solution)/shard_map/ppermute | solution.py:543
  159.0 51.6 %all-to-all-start.1 = ((bf16[8,208,512]{2,1,0:T(8,128)(2,1)}), bf16[8,208,512]{2,1,0:T(8,128)(2,1)S(1)}, u32[]{:S(2)}, u32[]{:S(2)}) async-start(bf16[8,208,512]{2,1,0:T(8,128)(2,1)} %shard_map.196), calls=%async_computation.1 | async-start | bytes 3407872 | tf_op jit(solution)/shard_map/all_to_all | solution.py:778
  171.9 26.7 %collective-permute-start.36 = (bf16[128,2048]{1,0:T(8,128)(2,1)}, bf16[128,2048]{1,0:T(8,128)(2,1)S(1)}, u32[]{:S(2)}, u32[]{:S(2)}) collective-permute-start(bf16[128,2048]{1,0:T(8,128)(2,1)} %get-tuple-element.223.refs_0_), channel_id=1, source_target_pairs={{0,2},{1,3},{2,0},{3,1},{4,6},{5,7},{6,4},{7,5},{8,10},{9,11},{10,... | collective-permute-start | bytes 1572872 | tf_op jit(solution)/shard_map/ppermute | solution.py:543
  173.4 26.0 %collective-permute-start.37 = (bf16[128,2048]{1,0:T(8,128)(2,1)}, bf16[128,2048]{1,0:T(8,128)(2,1)S(1)}, u32[]{:S(2)}, u32[]{:S(2)}) collective-permute-start(bf16[128,2048]{1,0:T(8,128)(2,1)} %get-tuple-element.199.refs_1_), channel_id=1, source_target_pairs={{0,2},{1,3},{2,0},{3,1},{4,6},{5,7},{6,4},{7,5},{8,10},{9,11},{10,... | collective-permute-start | bytes 1572872 | tf_op jit(solution)/shard_map/ppermute | solution.py:543
  211.8 46.8 %all-to-all-start.2 = ((bf16[8,96,2048]{2,1,0:T(8,128)(2,1)}), bf16[8,96,2048]{2,1,0:T(8,128)(2,1)S(1)}, u32[]{:S(2)}, u32[]{:S(2)}) async-start(bf16[8,96,2048]{2,1,0:T(8,128)(2,1)} %shard_map.203), calls=%async_computation.2 | async-start | bytes 6291456 | tf_op jit(solution)/shard_map/all_to_all | solution.py:577
  259.7 28.3 %all-to-all-start.3 = ((bf16[8,32,2176]{2,1,0:T(8,128)(2,1)}), bf16[8,32,2176]{2,1,0:T(8,128)(2,1)S(1)}, u32[]{:S(2)}, u32[]{:S(2)}) async-start(bf16[8,32,2176]{2,1,0:T(8,128)(2,1)} %shard_map.205), calls=%async_computation.3 | async-start | bytes 2228224 | tf_op jit(solution)/shard_map/all_to_all | solution.py:577
  265.6 19.6 %collective-permute-start.41 = (bf16[96,2048]{1,0:T(8,128)(2,1)S(1)}, bf16[96,2048]{1,0:T(8,128)(2,1)S(1)}, u32[]{:S(2)}, u32[]{:S(2)}) collective-permute-start(bf16[96,2048]{1,0:T(8,128)(2,1)S(1)} %copy-done.35), channel_id=1, source_target_pairs={{0,16},{4,20},{8,24},{12,28},{16,0},{20,4},{24,8},{28,12},{1,17},{... | collective-permute-start | bytes 1179656 | tf_op jit(solution)/shard_map/ppermute | solution.py:543
  288.8 25.1 %collective-permute-start.44 = (bf16[256,2048]{1,0:T(8,128)(2,1)S(1)}, bf16[256,2048]{1,0:T(8,128)(2,1)S(1)}, u32[]{:S(2)}, u32[]{:S(2)}) collective-permute-start(bf16[256,2048]{1,0:T(8,128)(2,1)S(1)} %copy-done.14), channel_id=1, source_target_pairs={{0,2},{1,3},{2,0},{3,1},{4,6},{5,7},{6,4},{7,5},{8,10},{9,11},{10,... | collective-permute-start | bytes 3145736 | tf_op jit(solution)/shard_map/ppermute | solution.py:543
  290.3 23.1 %collective-permute-start.45 = (bf16[96,2048]{1,0:T(8,128)(2,1)}, bf16[96,2048]{1,0:T(8,128)(2,1)S(1)}, u32[]{:S(2)}, u32[]{:S(2)}) collective-permute-start(bf16[96,2048]{1,0:T(8,128)(2,1)} %shard_map.211.refs_4_.refs_0_), channel_id=1, source_target_pairs={{0,4},{4,0},{8,12},{12,8},{16,20},{20,16},{24,28},{28,24},{1,5},{5... | collective-permute-start | bytes 1179656 | tf_op jit(solution)/shard_map/ppermute | solution.py:543
  291.8 21.6 %collective-permute-start.46 = (bf16[96,2048]{1,0:T(8,128)(2,1)}, bf16[96,2048]{1,0:T(8,128)(2,1)S(1)}, u32[]{:S(2)}, u32[]{:S(2)}) collective-permute-start(bf16[96,2048]{1,0:T(8,128)(2,1)} %shard_map.211.refs_4_.refs_0_), channel_id=1, source_target_pairs={{0,8},{4,12},{8,0},{12,4},{16,24},{20,28},{24,16},{28,20},{1,9},{5... | collective-permute-start | bytes 1179656 | tf_op jit(solution)/shard_map/ppermute | solution.py:543
  294.2 19.7 %collective-permute-start.47 = (bf16[96,2048]{1,0:T(8,128)(2,1)}, bf16[96,2048]{1,0:T(8,128)(2,1)S(1)}, u32[]{:S(2)}, u32[]{:S(2)}) collective-permute-start(bf16[96,2048]{1,0:T(8,128)(2,1)} %shard_map.211.refs_4_.refs_0_), channel_id=1, source_target_pairs={{0,12},{4,8},{8,4},{12,0},{16,28},{20,24},{24,20},{28,16},{1,13},{... | collective-permute-start | bytes 1179656 | tf_op jit(solution)/shard_map/ppermute | solution.py:543
  294.2 18.5 %collective-permute-start.43 = (bf16[32,2176]{1,0:T(8,128)(2,1)S(1)}, bf16[32,2176]{1,0:T(8,128)(2,1)S(1)}, u32[]{:S(2)}, u32[]{:S(2)}) collective-permute-start(bf16[32,2176]{1,0:T(8,128)(2,1)S(1)} %copy-done.42), channel_id=1, source_target_pairs={{0,16},{4,20},{8,24},{12,28},{16,0},{20,4},{24,8},{28,12},{1,17},{... | collective-permute-start | bytes 417800 | tf_op jit(solution)/shard_map/ppermute | solution.py:543
  (120 other events, 1080.5 us)
